TPU v7x, 32 devices: a whole 2x2x4 slice. The times are simulated.
32 devices in a mesh: ctx: 16 (over z, x, core), grp: 2 (over y).
Axes of the slice: x: 2, y: 2, z: 4, core: 2. Of those that a mesh axis runs over, the one named last changes fastest.
Arguments:
- inputs_se: bfloat16 [3, 2048, 8192], P(None, 'ctx', 'grp'), may hold values from -6 to 6
- cotangent_se: bfloat16 [2048, 8192], P('ctx', 'grp'), may hold values from -6 to 6
- kernel_se: bfloat16 [512, 7], P('grp'), may hold values from -2 to 2
- skip_se: float32 [8192], P('grp'), may hold values from -4 to 4
- inputs_mr: bfloat16 [3, 2048, 8192], P(None, 'ctx', 'grp'), may hold values from -6 to 6
- kernel_mr: bfloat16 [512, 128], P('grp'), may hold values from -0.5 to 0.5
- skip_mr: float32 [8192], P('grp'), may hold values from -4 to 4
- out_weight: bfloat16 [8192, 4096], P('grp', 'ctx'), may hold values from -0.0625 to 0.0625
- cotangent_out: bfloat16 [2048, 4096], P('ctx', 'grp'), may hold values from -6 to 6
Outputs:
- mixed_se: bfloat16 [2048, 8192], P('ctx', 'grp')
- projected: bfloat16 [2048, 4096], P('ctx', 'grp')
- grad_inputs_se: bfloat16 [3, 2048, 8192], P(None, 'ctx', 'grp')
- grad_inputs_mr: bfloat16 [3, 2048, 8192], P(None, 'ctx', 'grp')
- grad_kernel_se: float32 [512, 7], P('grp')
- grad_kernel_mr: float32 [512, 128], P('grp')
- grad_skip_se: float32 [8192], P('grp')
- grad_skip_mr: float32 [8192], P('grp')
- grad_out_weight: float32 [8192, 4096], P('grp', 'ctx')
All inputs are finite; a program needn't handle non-finite values.
Results may differ from a plain program's by a relative error of at most 0.012.
Values may be sent and summed in bfloat16 or wider, within the bound.
A program may use at most 256 MiB of HBM per device.

v0:
```python
import jax
import jax.numpy as jnp
from jax import lax
from jax.sharding import PartitionSpec as P

GROUP = 16


HIGH = lax.Precision.HIGHEST


def tap_tables(length, tile_rows):
    table_shape = (tile_rows, tile_rows, length)
    row_ids = lax.broadcasted_iota(jnp.int32, table_shape, 0)
    col_ids = lax.broadcasted_iota(jnp.int32, table_shape, 1)
    tap_ids = lax.broadcasted_iota(jnp.int32, table_shape, 2)
    inside = (row_ids - col_ids == tap_ids).astype(jnp.bfloat16)
    across = (row_ids - col_ids + tile_rows == tap_ids).astype(jnp.bfloat16)
    return (inside, across)


def filter_blocks(kernel, tables):
    inside, across = tables
    near_band = jnp.einsum(
        "gs,ijs->gij", kernel, inside, preferred_element_type=jnp.float32
    ).astype(jnp.bfloat16)
    far_band = jnp.einsum("gs,ijs->gij", kernel, across, preferred_element_type=jnp.float32).astype(
        jnp.bfloat16
    )
    return (near_band, far_band)


def gated_product(inputs):
    return (inputs[1].astype(jnp.float32) * inputs[2]).astype(jnp.bfloat16)


def gate_grad_of(upstream, inputs):
    return (upstream.astype(jnp.float32) * inputs[0]).astype(jnp.bfloat16)


def as_tiles(values, tile_rows):
    return values.reshape(values.shape[0] // tile_rows, tile_rows, values.shape[1] // GROUP, GROUP)


def forward(inputs, product, skip_scale, before, bands):
    near_band, far_band = bands
    tile_rows = near_band.shape[1]
    tiled = as_tiles(product, tile_rows)
    earlier = jnp.concatenate([as_tiles(before, tile_rows), tiled[:-1]], 0)
    convolved = jnp.einsum("gij,njgc->nigc", near_band, tiled, preferred_element_type=jnp.float32)
    convolved = convolved + jnp.einsum(
        "gij,njgc->nigc", far_band, earlier, preferred_element_type=jnp.float32
    )
    convolved = convolved.reshape(product.shape) + skip_scale * product.astype(jnp.float32)
    mixed = (inputs[0] * convolved).astype(jnp.bfloat16)
    return ((convolved, tiled, earlier), mixed)


def backward(inputs, product, state, upstream, gate_grad, after_rows, skip_scale, bands, tables):
    convolved, tiled, earlier = state
    near_band, far_band = bands
    inside, across = tables
    tile_rows = near_band.shape[1]
    grad_tiles = as_tiles(gate_grad, tile_rows)
    following = jnp.concatenate([grad_tiles[1:], as_tiles(after_rows, tile_rows)], 0)
    spread = jnp.einsum("gji,njgc->nigc", near_band, grad_tiles, preferred_element_type=jnp.float32)
    spread = spread + jnp.einsum(
        "gji,njgc->nigc", far_band, following, preferred_element_type=jnp.float32
    )
    spread = spread.reshape(product.shape) + skip_scale * gate_grad.astype(jnp.float32)
    grad_query = (upstream * convolved).astype(jnp.bfloat16)
    grad_key = (spread * inputs[2]).astype(jnp.bfloat16)
    grad_value = (spread * inputs[1]).astype(jnp.bfloat16)
    cross_near = jnp.einsum("nigc,njgc->gij", grad_tiles, tiled, preferred_element_type=jnp.float32)
    cross_far = jnp.einsum(
        "nigc,njgc->gij", grad_tiles, earlier, preferred_element_type=jnp.float32
    )
    grad_kernel = jnp.einsum("gij,ijs->gs", cross_near, inside.astype(jnp.float32), precision=HIGH)
    grad_kernel = grad_kernel + jnp.einsum(
        "gij,ijs->gs", cross_far, across.astype(jnp.float32), precision=HIGH
    )
    grad_skip = jnp.sum(gate_grad.astype(jnp.float32) * product.astype(jnp.float32), axis=0)
    return (jnp.stack([grad_query, grad_key, grad_value]), grad_kernel, grad_skip)


def project(mixed_mr, full_weight, cotangent_out):
    partial_value = jnp.dot(mixed_mr, full_weight, preferred_element_type=jnp.float32)
    projected = lax.psum_scatter(
        partial_value.astype(jnp.bfloat16), "grp", scatter_dimension=1, tiled=True
    )
    full_cotangent = lax.all_gather(cotangent_out, "grp", axis=1, tiled=True)
    upstream = lax.dot_general(
        full_cotangent, full_weight, (((1,), (1,)), ((), ())), preferred_element_type=jnp.float32
    ).astype(jnp.bfloat16)
    weight_share = lax.psum_scatter(
        lax.dot_general(
            full_cotangent, mixed_mr, (((0,), (0,)), ((), ())), preferred_element_type=jnp.float32
        ).astype(jnp.bfloat16),
        "ctx",
        scatter_dimension=0,
        tiled=True,
    ).astype(jnp.float32)
    return (projected, upstream, weight_share.T)


def on_device(
    inputs_se,
    cotangent_se,
    kernel_se,
    skip_se,
    inputs_mr,
    kernel_mr,
    skip_mr,
    out_weight,
    cotangent_out,
):
    tile_rows = kernel_mr.shape[1]
    length_se = kernel_se.shape[1]
    tables_se = tap_tables(length_se, tile_rows)
    tables_mr = tap_tables(tile_rows, tile_rows)
    full_weight = lax.all_gather(out_weight, "ctx", axis=1, tiled=True)
    moved_se, moved_cotangent, moved_mr = (
        lax.all_to_all(inputs_se, "ctx", split_axis=2, concat_axis=1, tiled=True),
        lax.all_to_all(cotangent_se[None], "ctx", split_axis=2, concat_axis=1, tiled=True),
        lax.all_to_all(inputs_mr, "ctx", split_axis=2, concat_axis=1, tiled=True),
    )
    channels = moved_se.shape[2]
    groups = channels // GROUP
    first_group = lax.axis_index("ctx") * groups
    kernel_slice_se = lax.dynamic_slice_in_dim(kernel_se, first_group, groups, 0)
    kernel_slice_mr = lax.dynamic_slice_in_dim(kernel_mr, first_group, groups, 0)
    skip_slice_se = lax.dynamic_slice_in_dim(skip_se, first_group * GROUP, channels, 0)
    skip_slice_mr = lax.dynamic_slice_in_dim(skip_mr, first_group * GROUP, channels, 0)
    blank_rows = jnp.zeros((tile_rows, channels), jnp.bfloat16)
    bands_se = filter_blocks(kernel_slice_se, tables_se)
    bands_mr = filter_blocks(kernel_slice_mr, tables_mr)
    product_se = gated_product(moved_se)
    state_se, local_mixed_se = forward(moved_se, product_se, skip_slice_se, blank_rows, bands_se)
    gate_se = gate_grad_of(moved_cotangent[0], moved_se)
    local_grads_se, kernel_part_se, skip_part_se = backward(
        moved_se,
        product_se,
        state_se,
        moved_cotangent[0],
        gate_se,
        blank_rows,
        skip_slice_se,
        bands_se,
        tables_se,
    )
    product_mr = gated_product(moved_mr)
    state_mr, local_mixed_mr = forward(moved_mr, product_mr, skip_slice_mr, blank_rows, bands_mr)
    mixed_back_se, grad_inputs_se, mixed_back_mr = (
        lax.all_to_all(local_mixed_se[None], "ctx", split_axis=1, concat_axis=2, tiled=True),
        lax.all_to_all(local_grads_se, "ctx", split_axis=1, concat_axis=2, tiled=True),
        lax.all_to_all(local_mixed_mr[None], "ctx", split_axis=1, concat_axis=2, tiled=True),
    )
    mixed_se = mixed_back_se[0]
    projected, upstream_mr, grad_out_weight = project(mixed_back_mr[0], full_weight, cotangent_out)
    moved_upstream = lax.all_to_all(
        upstream_mr[None], "ctx", split_axis=2, concat_axis=1, tiled=True
    )[0]
    gate_mr = gate_grad_of(moved_upstream, moved_mr)
    local_grads_mr, kernel_part_mr, skip_part_mr = backward(
        moved_mr,
        product_mr,
        state_mr,
        moved_upstream,
        gate_mr,
        blank_rows,
        skip_slice_mr,
        bands_mr,
        tables_mr,
    )
    grad_inputs_mr = lax.all_to_all(local_grads_mr, "ctx", split_axis=1, concat_axis=2, tiled=True)
    grad_kernel_se, grad_kernel_mr, grad_skip_se, grad_skip_mr = (
        lax.all_gather(kernel_part_se, "ctx", axis=0, tiled=True),
        lax.all_gather(kernel_part_mr, "ctx", axis=0, tiled=True),
        lax.all_gather(skip_part_se, "ctx", axis=0, tiled=True),
        lax.all_gather(skip_part_mr, "ctx", axis=0, tiled=True),
    )
    return (
        mixed_se,
        projected,
        grad_inputs_se,
        grad_inputs_mr,
        grad_kernel_se,
        grad_kernel_mr,
        grad_skip_se,
        grad_skip_mr,
        grad_out_weight,
    )


def solution(mesh):
    placed = (
        P(None, "ctx", "grp"),
        P("ctx", "grp"),
        P("grp", None),
        P("grp"),
        P(None, "ctx", "grp"),
        P("grp", None),
        P("grp"),
        P("grp", "ctx"),
        P("ctx", "grp"),
    )
    return jax.shard_map(
        on_device,
        mesh=mesh,
        in_specs=placed,
        out_specs=(
            P("ctx", "grp"),
            P("ctx", "grp"),
            P(None, "ctx", "grp"),
            P(None, "ctx", "grp"),
            P("grp", None),
            P("grp", None),
            P("grp"),
            P("grp"),
            P("grp", "ctx"),
        ),
        check_vma=False,
    )
```

profile of v0, /device:TPU:0, one launch (start us, length us, event | category | flops | bytes accessed | tf_op | source)
XLA Modules:
  0.0 1205.2 jit_solution(6193755338356854701)
XLA Ops:
  23.2 10.4 all-gather.8.cloned.1.call-done
  33.6 252.2 %all-gather.6.cloned.1.call-done = bf16[4096,4096]{1,0:T(8,128)(2,1)} async-done(((bf16[4096,256]{1,0:T(8,128)(2,1)}), bf16[4096,4096]{1,0:T(8,128)(2,1)}) %all-gather.6.cloned.1.call-update) | async-done | bytes 33554448 | tf_op jit(solution)/shard_map/all_gather | solution.py:121
  285.8 16.2 %fusion.4 = bf16[1,128,4096]{2,1,0:T(8,128)(2,1)S(1)} fusion(bf16[128,4096]{1,0:T(8,128)(2,1)} %all-gather.8.cloned.1.call-done, bf16[4096,4096]{1,0:T(8,128)(2,1)} %all-gather.6.cloned.1.call-done), kind=kOutput, calls=%fused_computation.10 | convolution fusion | flops 4295491584 | bytes 35651584 | tf_op jit(solution)/shard_map/dot_general | solution.py:92
  305.3 22.4 %reduce.4 = bf16[4096,128]{1,0:T(8,128)(2,1)S(1)} reduce(bf16[4096,1,128]{2,1,0:T(2,128)(2,1)S(1)} %bitcast.231, bf16[]{:T(256)} %broadcast.181), dimensions={1}, to_apply=%bitcast.176.reduce_sub_computation | reduce | bytes 2097154
  395.3 11.6 copy.299
  406.9 10.6 reduce.5
  418.2 31.5 %all_to_all.114 = bf16[16,2,16384]{2,1,0:T(2,128)(2,1)S(1)} all-to-all(bf16[16,2,16384]{2,1,0:T(2,128)(2,1)S(1)} %reshape.644), channel_id=1, replica_groups=mesh['ctx'=16,'grp'=2] {'ctx'}, dimensions={0} | all-to-all | bytes 2097152 | tf_op jit(solution)/shard_map/all_to_all | solution.py:156
  453.6 14.3 %convert_bitcast_fusion = bf16[4096,4096]{0,1:T(8,128)(2,1)} fusion(bf16[128,4096]{0,1:T(8,128)(2,1)S(1)} %bitcast.217, bf16[128,4096]{1,0:T(8,128)(2,1)S(1)} %copy-done.25), kind=kOutput, calls=%fused_computation | convolution fusion | flops 4311744512 | bytes 35651584 | tf_op jit(solution)/shard_map/dot_general | solution.py:96
  471.9 22.4 %reduce.2 = bf16[4096,128]{1,0:T(8,128)(2,1)S(1)} reduce(bf16[4096,1,128]{2,1,0:T(2,128)(2,1)S(1)} %bitcast.234, bf16[]{:T(256)} %broadcast.181), dimensions={1}, to_apply=%bitcast.174.reduce_sub_computation | reduce | bytes 2097154
  500.4 7.5 copy.169
  507.9 15.4 %all-to-all-done.4 = bf16[16,2,16384]{2,1,0:T(2,128)(2,1)S(1)} async-done(((bf16[16,2,16384]{2,1,0:T(2,128)(2,1)}), bf16[16,2,16384]{2,1,0:T(2,128)(2,1)S(1)}, u32[]{:S(2)}, u32[]{:S(2)}) %all-to-all-start.4) | async-done | bytes 1048608 | tf_op jit(solution)/shard_map/all_to_all | solution.py:124
  540.2 128.1 %all-to-all-done = bf16[3,128,4096]{1,0,2:T(4,128)(2,1)} async-done(((bf16[3,128,4096]{1,0,2:T(4,128)(2,1)}), bf16[3,128,4096]{1,0,2:T(4,128)(2,1)}, u32[]{:S(2)}, u32[]{:S(2)}) %all-to-all-start) | async-done | bytes 3145760 | tf_op jit(solution)/shard_map/all_to_all | solution.py:123
  712.4 11.6 copy.300
  724.1 10.8 reduce.3
  736.1 53.3 %all-to-all-start.1 = ((bf16[16,2,16384]{2,1,0:T(2,128)(2,1)}), bf16[16,2,16384]{2,1,0:T(2,128)(2,1)S(1)}, u32[]{:S(2)}, u32[]{:S(2)}) async-start(bf16[16,2,16384]{2,1,0:T(2,128)(2,1)} %reshape.642), calls=%async_computation.1 | async-start | bytes 2097152 | tf_op jit(solution)/shard_map/all_to_all | solution.py:154
  791.0 17.1 %copy.204 = bf16[3,2048,256]{2,0,1:T(4,128)(2,1)} copy(bf16[3,2048,256]{2,1,0:T(8,128)(2,1)S(1)} %pad_maximum_fusion) | data formatting | bytes 6291456 | tf_op jit(solution)/shard_map/stack | solution.py:83
  821.3 17.2 %copy.215 = bf16[3,2048,256]{2,0,1:T(4,128)(2,1)} copy(bf16[3,2048,256]{2,1,0:T(8,128)(2,1)S(1)} %pad_maximum_fusion.1) | data formatting | bytes 6291456 | tf_op jit(solution)/shard_map/stack | solution.py:83
  838.5 113.4 %all-to-all-done.5 = bf16[3,2048,256]{2,0,1:T(4,128)(2,1)} async-done(((bf16[3,2048,256]{2,0,1:T(4,128)(2,1)}), bf16[3,2048,256]{2,0,1:T(4,128)(2,1)}, u32[]{:S(2)}, u32[]{:S(2)}) %all-to-all-start.5) | async-done | bytes 3145760 | tf_op jit(solution)/shard_map/all_to_all | solution.py:155
  951.9 32.4 %all-to-all-start.7 = ((bf16[3,2048,256]{2,0,1:T(4,128)(2,1)}), bf16[3,2048,256]{2,0,1:T(4,128)(2,1)}, u32[]{:S(2)}, u32[]{:S(2)}) async-start(bf16[3,2048,256]{2,0,1:T(4,128)(2,1)} %copy.215), calls=%async_computation.8 | async-start | bytes 8388608 | tf_op jit(solution)/shard_map/all_to_all | solution.py:175
  984.4 83.9 %all-gather.1 = f32[16,1,256]{2,1,0:T(1,128)S(1)} all-gather(f32[1,1,256]{2,1,0:T(1,128)S(1)} %bitcast.248), channel_id=1, replica_groups=mesh['ctx'=16,'grp'=2] {'ctx'}, dimensions={0}, use_global_device_ids=true | all-gather | bytes 17408 | tf_op jit(solution)/shard_map/all_gather | solution.py:179
  1072.0 38.6 %all-gather = f32[16,16,7]{1,2,0:T(8,128)S(1)} all-gather(f32[1,16,7]{1,2,0:T(8,128)S(1)} %fusion.29), channel_id=1, replica_groups=mesh['ctx'=16,'grp'=2] {'ctx'}, dimensions={0}, use_global_device_ids=true | all-gather | bytes 7616 | tf_op jit(solution)/shard_map/all_gather | solution.py:177
  1124.8 14.2 %convolution_convert_fusion.1 = bf16[128,4096]{1,0:T(8,128)(2,1)} fusion(bf16[128,4096]{0,1:T(8,128)(2,1)S(1)} %bitcast.218, bf16[4096,4096]{1,0:T(8,128)(2,1)} %all-gather.6.cloned.1.call-done), kind=kOutput, calls=%fused_computation.9 | convolution fusion | flops 4295491584 | bytes 35651584 | tf_op jit(solution)/shard_map/dot_general | solution.py:87
  1139.6 17.4 %all-gather.2 = f32[16,1,256]{2,1,0:T(1,128)S(1)} all-gather(f32[1,1,256]{2,1,0:T(1,128)S(1)} %bitcast.249), channel_id=1, replica_groups=mesh['ctx'=16,'grp'=2] {'ctx'}, dimensions={0}, use_global_device_ids=true | all-gather | bytes 17408 | tf_op jit(solution)/shard_map/all_gather | solution.py:180
  1163.5 19.1 %all_gather.21 = f32[256,128]{1,0:T(8,128)S(1)} all-gather(f32[16,128]{1,0:T(8,128)S(1)} %fusion.27), channel_id=1, replica_groups=mesh['ctx'=16,'grp'=2] {'ctx'}, dimensions={0}, use_global_device_ids=true | all-gather | bytes 139264 | tf_op jit(solution)/shard_map/all_gather | solution.py:178
  (193 shorter events, 218.8 us)
Async XLA Ops:
  7.2 327.0 %copy-start = (bf16[256,128]{1,0:T(8,128)(2,1)S(1)}, bf16[256,128]{1,0:T(8,128)(2,1)}, u32[]{:S(2)}) copy-start(bf16[256,128]{1,0:T(8,128)(2,1)} %param.14) | copy-start | bytes 196612
  7.2 26.4 %all-gather.8.cloned.1.call-start = ((), (), s32[]{:S(2)}) async-start(), calls=%async_computation.12 | async-start | bytes 1572864 | tf_op jit(solution)/shard_map/all_gather | solution.py:91
  7.9 277.9 %all-gather.6.cloned.1.call-start = ((), (), s32[]{:S(2)}) async-start(), calls=%async_computation.10 | async-start | bytes 35651584 | tf_op jit(solution)/shard_map/all_gather | solution.py:121
  15.8 313.0 %all-to-all-start.2 = ((bf16[3,128,4096]{1,0,2:T(4,128)(2,1)}), bf16[3,128,4096]{1,0,2:T(4,128)(2,1)}, u32[]{:S(2)}, u32[]{:S(2)}) async-start(bf16[3,128,4096]{1,0,2:T(4,128)(2,1)} %copy.182), calls=%async_computation.2 | async-start | bytes 8388608 | tf_op jit(solution)/shard_map/all_to_all | solution.py:125
  328.8 27.3 %all-to-all-start.6 = ((bf16[16,2,16384]{2,1,0:T(2,128)(2,1)}), bf16[16,2,16384]{2,1,0:T(2,128)(2,1)}, u32[]{:S(2)}, u32[]{:S(2)}) async-start(bf16[16,2,16384]{2,1,0:T(2,128)(2,1)} %reshape.648), calls=%async_computation.7 | async-start | bytes 2097152 | tf_op jit(solution)/shard_map/all_to_all | solution.py:160
  333.2 859.5 %reduce-scatter.5.cloned.1.call-start = ((), (), s32[]{:S(2)}) async-start(), calls=%async_computation.13 | async-start | bytes 35651584 | tf_op jit(solution)/shard_map/reduce_scatter | solution.py:95
  453.5 14.3 %copy-start.10 = (bf16[1,128,16,256]{1,3,2,0:T(8,128)(2,1)}, bf16[1,128,16,256]{1,3,2,0:T(8,128)(2,1)S(1)}, u32[]{:S(2)}) copy-start(bf16[1,128,16,256]{1,3,2,0:T(8,128)(2,1)S(1)} %copy.194) | copy-start | bytes 3145732
  495.4 27.9 %all-to-all-start.4 = ((bf16[16,2,16384]{2,1,0:T(2,128)(2,1)}), bf16[16,2,16384]{2,1,0:T(2,128)(2,1)S(1)}, u32[]{:S(2)}, u32[]{:S(2)}) async-start(bf16[16,2,16384]{2,1,0:T(2,128)(2,1)} %reshape.646), calls=%async_computation.5 | async-start | bytes 2097152 | tf_op jit(solution)/shard_map/all_to_all | solution.py:124
  507.9 23.3 %copy-start.41 = (bf16[256,7]{0,1:T(8,128)(2,1)S(1)}, bf16[256,7]{0,1:T(8,128)(2,1)}, u32[]{:S(2)}) copy-start(bf16[256,7]{0,1:T(8,128)(2,1)} %param.11) | copy-start | bytes 10756
  523.3 144.9 %all-to-all-start = ((bf16[3,128,4096]{1,0,2:T(4,128)(2,1)}), bf16[3,128,4096]{1,0,2:T(4,128)(2,1)}, u32[]{:S(2)}, u32[]{:S(2)}) async-start(bf16[3,128,4096]{1,0,2:T(4,128)(2,1)} %copy.169), calls=%async_computation | async-start | bytes 8388608 | tf_op jit(solution)/shard_map/all_to_all | solution.py:123
  703.7 6.7 copy-start.7
  734.9 54.5 %copy-start.28 = (bf16[1,2048,256]{2,1,0:T(8,128)(2,1)S(1)}, bf16[1,2048,256]{2,1,0:T(8,128)(2,1)}, u32[]{:S(2)}) copy-start(bf16[1,2048,256]{2,1,0:T(8,128)(2,1)} %get-tuple-element.48) | copy-start | bytes 3145732
  734.9 54.5 %copy-start.29 = (bf16[1,2048,256]{2,1,0:T(8,128)(2,1)S(1)}, bf16[1,2048,256]{2,1,0:T(8,128)(2,1)}, u32[]{:S(2)}) copy-start(bf16[1,2048,256]{2,1,0:T(8,128)(2,1)} %get-tuple-element.52) | copy-start | bytes 3145732
  736.1 76.3 %all-to-all-start.1 = ((bf16[16,2,16384]{2,1,0:T(2,128)(2,1)}), bf16[16,2,16384]{2,1,0:T(2,128)(2,1)S(1)}, u32[]{:S(2)}, u32[]{:S(2)}) async-start(bf16[16,2,16384]{2,1,0:T(2,128)(2,1)} %reshape.642), calls=%async_computation.1 | async-start | bytes 2097152 | tf_op jit(solution)/shard_map/all_to_all | solution.py:154
  808.1 11.6 copy-start.26
  808.1 11.6 copy-start.27
  812.4 139.5 %all-to-all-start.5 = ((bf16[3,2048,256]{2,0,1:T(4,128)(2,1)}), bf16[3,2048,256]{2,0,1:T(4,128)(2,1)}, u32[]{:S(2)}, u32[]{:S(2)}) async-start(bf16[3,2048,256]{2,0,1:T(4,128)(2,1)} %copy.204), calls=%async_computation.6 | async-start | bytes 8388608 | tf_op jit(solution)/shard_map/all_to_all | solution.py:155
  838.5 229.9 %copy-start.18 = (bf16[1,16,128,256]{2,3,1,0:T(8,128)(2,1)S(1)}, bf16[1,16,128,256]{2,3,1,0:T(8,128)(2,1)}, u32[]{:S(2)}) copy-start(bf16[1,16,128,256]{2,3,1,0:T(8,128)(2,1)} %copy-done.17) | copy-start | bytes 3145732
  838.5 229.9 %copy-start.20 = (bf16[1,16,128,256]{2,3,1,0:T(8,128)(2,1)S(1)}, bf16[1,16,128,256]{2,3,1,0:T(8,128)(2,1)}, u32[]{:S(2)}) copy-start(bf16[1,16,128,256]{2,3,1,0:T(8,128)(2,1)} %copy-done.19) | copy-start | bytes 3145732
  951.9 230.7 %all-to-all-start.7 = ((bf16[3,2048,256]{2,0,1:T(4,128)(2,1)}), bf16[3,2048,256]{2,0,1:T(4,128)(2,1)}, u32[]{:S(2)}, u32[]{:S(2)}) async-start(bf16[3,2048,256]{2,0,1:T(4,128)(2,1)} %copy.215), calls=%async_computation.8 | async-start | bytes 8388608 | tf_op jit(solution)/shard_map/all_to_all | solution.py:175
  984.4 212.2 %reduce-scatter.3.cloned.1.call-start = ((), (), s32[]{:S(2)}) async-start(), calls=%async_computation.11 | async-start | bytes 1572864 | tf_op jit(solution)/shard_map/reduce_scatter | solution.py:88
  1124.8 14.2 %copy-start.14 = (bf16[1,16,128,256]{2,3,1,0:T(8,128)(2,1)S(1)}, bf16[1,16,128,256]{2,3,1,0:T(8,128)(2,1)}, u32[]{:S(2)}) copy-start(bf16[1,16,128,256]{2,3,1,0:T(8,128)(2,1)} %copy-done.12) | copy-start | bytes 3145732
  1124.8 14.2 %copy-start.32 = (bf16[1,15,128,256]{2,3,1,0:T(8,128)(2,1)S(1)}, bf16[1,15,128,256]{2,3,1,0:T(8,128)(2,1)}, u32[]{:S(2)}) copy-start(bf16[1,15,128,256]{2,3,1,0:T(8,128)(2,1)} %copy-done.31) | copy-start | bytes 2949124
  1188.0 10.5 copy-start.1
  (29 other events, 87.2 us)
Sparse Core Ops, SparseCore 0:
  9.6 23.9 all-gather.7
  35.1 250.6 all-gather.5
  468.0 504.2 reduce-scatter.4
  1139.2 17.0 reduce-scatter.2
where the time goes:
time: 1220 us; the launch traced here: 1210 us
  waiting for transfers between devices  528 us (43%)
  blocking collectives  191 us (16%)
  local copies, waits for them, and re-layouts  181 us (15%)
  starting transfers between devices  117 us (10%)
  other arithmetic  106 us (9%)
  matrix products  67.3 us (6%)
  between operations  14.6 us (1%)
    all_gather x1, waiting for transfers between devices, on_device(): full_weight = lax.all_gather(out_weight, 'ctx', axis=1, tiled=True)  252 us
    all_to_all x1, waiting for transfers between devices, on_device(): lax.all_to_all(inputs_se, 'ctx', split_axis=2, concat_axis=1, tiled=True)  128 us
    all_to_all x1, waiting for transfers between devices, on_device(): lax.all_to_all(local_grads_se, 'ctx', split_axis=1, concat_axis=2, tiled=...  113 us
    all_gather x1, blocking collectives, on_device(): lax.all_gather(skip_part_se, 'ctx', axis=0, tiled=True)  83.9 us
    unnamed x4, other arithmetic  66.2 us
    all_to_all x1, starting transfers between devices, on_device(): lax.all_to_all(local_mixed_se[None], 'ctx', split_axis=1, concat_axis=2,...  53.3 us
    unnamed x104, local copies, waits for them, and re-layouts  47.2 us
    all_gather x1, blocking collectives, on_device(): lax.all_gather(kernel_part_se, 'ctx', axis=0, tiled=True)  38.6 us
  transfers between devices with their start and end apart: 11, of which 7 were waited for; matrix products, arithmetic and copies ran while one was open for 22% of the time, Pallas kernels for 0%

commit v1 on v0

v1 whole, which is shorter than its diff:
```python
import jax
import jax.numpy as jnp
from jax import lax
from jax.experimental import pallas as pl
from jax.experimental.pallas import tpu as pltpu
from jax.sharding import PartitionSpec as P

GROUP = 16
LANES = 256
F32 = jnp.float32
BF16 = jnp.bfloat16


def lane_group(rows):
    return lax.broadcasted_iota(jnp.int32, (rows, LANES), 1) // GROUP


def banded(base_ref, data, taps):
    owner = lane_group(taps)
    total = jnp.zeros((taps, LANES), F32)
    for g in range(LANES // GROUP):
        row = jnp.broadcast_to(base_ref[g : g + 1, :], (taps, 2 * taps))
        band = pltpu.roll(row, 0, 1, stride=1, stride_axis=0).astype(BF16)
        part = jnp.dot(band, data, preferred_element_type=F32)
        total = jnp.where(owner == g, part, total)
    return total


def mr_forward_kernel(inputs_ref, before_ref, base_ref, skip_ref, conv_ref, mixed_ref):
    taps = before_ref.shape[0]
    product = (inputs_ref[1].astype(F32) * inputs_ref[2].astype(F32)).astype(BF16)
    data = jnp.concatenate([before_ref[...], product], 0)
    conv = banded(base_ref, data, taps) + skip_ref[...] * product.astype(F32)
    conv_ref[...] = conv
    mixed_ref[...] = (inputs_ref[0].astype(F32) * conv).astype(BF16)


def mr_forward(inputs, before, base, skip):
    _, rows, channels = inputs.shape
    return pl.pallas_call(
        mr_forward_kernel,
        grid=(channels // LANES,),
        in_specs=[
            pl.BlockSpec((3, rows, LANES), lambda i: (0, 0, i)),
            pl.BlockSpec((rows, LANES), lambda i: (0, i)),
            pl.BlockSpec((LANES // GROUP, 2 * rows), lambda i: (i, 0)),
            pl.BlockSpec((1, LANES), lambda i: (0, i)),
        ],
        out_specs=[
            pl.BlockSpec((rows, LANES), lambda i: (0, i)),
            pl.BlockSpec((rows, LANES), lambda i: (0, i)),
        ],
        out_shape=[
            jax.ShapeDtypeStruct((rows, channels), F32),
            jax.ShapeDtypeStruct((rows, channels), BF16),
        ],
        compiler_params=pltpu.CompilerParams(vmem_limit_bytes=32 * 2**20),
        cost_estimate=pl.CostEstimate(
            flops=4 * rows * rows * channels * GROUP, bytes_accessed=11 * rows * channels,
            transcendentals=0,
        ),
        name="mr_forward",
    )(inputs, before, base, skip)


def mr_backward_kernel(
    inputs_ref, before_ref, upstream_ref, after_ref, conv_ref, base_ref, skip_ref,
    grads_ref, cross_ref, skip_grad_ref,
):
    taps = before_ref.shape[0]
    product = (inputs_ref[1].astype(F32) * inputs_ref[2].astype(F32)).astype(BF16)
    data = jnp.concatenate([before_ref[...], product], 0)
    upstream = upstream_ref[...].astype(F32)
    gate = (upstream * inputs_ref[0].astype(F32)).astype(BF16)
    gate_f = gate.astype(F32)
    spread = banded(base_ref, jnp.concatenate([gate, after_ref[...]], 0), taps)
    spread = spread + skip_ref[...] * gate_f
    grads_ref[0] = (upstream * conv_ref[...]).astype(BF16)
    grads_ref[1] = (spread * inputs_ref[2].astype(F32)).astype(BF16)
    grads_ref[2] = (spread * inputs_ref[1].astype(F32)).astype(BF16)
    skip_grad_ref[...] = jnp.sum(gate_f * product.astype(F32), axis=0, keepdims=True)
    owner = lane_group(taps)
    for g in range(LANES // GROUP):
        kept = jnp.where(owner == g, gate_f, 0.0).astype(BF16)
        cross = lax.dot_general(
            kept, data, (((1,), (1,)), ((), ())), preferred_element_type=F32
        )
        total = cross[0:8]
        for a in range(1, taps // 8):
            total = total + pltpu.roll(cross[8 * a : 8 * a + 8], 2 * taps - 8 * a, 1)
        cross_ref[g] = total


def mr_backward(inputs, before, upstream, after, conv, base, skip):
    _, rows, channels = inputs.shape
    flat = pl.BlockSpec((rows, LANES), lambda i: (0, i))
    cube = pl.BlockSpec((3, rows, LANES), lambda i: (0, 0, i))
    line = pl.BlockSpec((1, LANES), lambda i: (0, i))
    return pl.pallas_call(
        mr_backward_kernel,
        grid=(channels // LANES,),
        in_specs=[
            cube, flat, flat, flat, flat,
            pl.BlockSpec((LANES // GROUP, 2 * rows), lambda i: (i, 0)),
            line,
        ],
        out_specs=[
            cube,
            pl.BlockSpec((LANES // GROUP, 8, 2 * rows), lambda i: (i, 0, 0)),
            line,
        ],
        out_shape=[
            jax.ShapeDtypeStruct((3, rows, channels), BF16),
            jax.ShapeDtypeStruct((channels // GROUP, 8, 2 * rows), F32),
            jax.ShapeDtypeStruct((1, channels), F32),
        ],
        compiler_params=pltpu.CompilerParams(vmem_limit_bytes=32 * 2**20),
        cost_estimate=pl.CostEstimate(
            flops=8 * rows * rows * channels * GROUP, bytes_accessed=24 * rows * channels,
            transcendentals=0,
        ),
        name="mr_backward",
    )(inputs, before, upstream, after, conv, base, skip)


def se_kernel(
    taps, inputs_ref, cotangent_ref, before_ref, after_ref, filter_ref, skip_ref,
    mixed_ref, grads_ref, sums_ref,
):
    rows = cotangent_ref.shape[0]
    query = inputs_ref[0].astype(F32)
    cotangent = cotangent_ref[...].astype(F32)
    key = inputs_ref[1].astype(F32)
    value = inputs_ref[2].astype(F32)
    product = (key * value).astype(BF16).astype(F32)
    gate = (cotangent * query).astype(BF16).astype(F32)
    earlier = jnp.concatenate([before_ref[...], product], 0)
    later = jnp.concatenate([gate, after_ref[...]], 0)
    pad = before_ref.shape[0]
    conv = skip_ref[...] * product
    spread = skip_ref[...] * gate
    sums = []
    for s in range(taps):
        weight = filter_ref[s : s + 1, :]
        moved = earlier[pad - s : pad - s + rows]
        conv = conv + weight * moved
        spread = spread + weight * later[s : s + rows]
        sums.append(jnp.sum(gate * moved, axis=0, keepdims=True))
    sums.append(jnp.zeros((sums_ref.shape[0] - taps, sums[0].shape[1]), F32))
    sums_ref[...] = jnp.concatenate(sums, 0)
    mixed_ref[...] = (query * conv).astype(BF16)
    grads_ref[0] = (cotangent * conv).astype(BF16)
    grads_ref[1] = (spread * value).astype(BF16)
    grads_ref[2] = (spread * key).astype(BF16)


def se_operator(inputs, cotangent, before, after, filters, skip, taps):
    _, rows, channels = inputs.shape
    halo = before.shape[0]
    flat = pl.BlockSpec((rows, LANES), lambda i: (0, i))
    cube = pl.BlockSpec((3, rows, LANES), lambda i: (0, 0, i))
    line = pl.BlockSpec((1, LANES), lambda i: (0, i))
    edge = pl.BlockSpec((halo, LANES), lambda i: (0, i))

    def kernel(*refs):
        se_kernel(taps, *refs)

    return pl.pallas_call(
        kernel,
        grid=(channels // LANES,),
        in_specs=[cube, flat, edge, edge, edge, line],
        out_specs=[flat, cube, edge],
        out_shape=[
            jax.ShapeDtypeStruct((rows, channels), BF16),
            jax.ShapeDtypeStruct((3, rows, channels), BF16),
            jax.ShapeDtypeStruct((halo, channels), F32),
        ],
        compiler_params=pltpu.CompilerParams(vmem_limit_bytes=32 * 2**20),
        cost_estimate=pl.CostEstimate(
            flops=50 * rows * channels, bytes_accessed=16 * rows * channels, transcendentals=0
        ),
        name="se_operator",
    )(inputs, cotangent, before, after, filters, skip)


def gated(left, right):
    return (left.astype(F32) * right.astype(F32)).astype(BF16)


def on_device(
    inputs_se, cotangent_se, kernel_se, skip_se, inputs_mr, kernel_mr, skip_mr, out_weight,
    cotangent_out,
):
    count = lax.axis_size("ctx")
    up = [(i, i + 1) for i in range(count - 1)]
    down = [(i + 1, i) for i in range(count - 1)]
    rows = inputs_mr.shape[1]
    channels = inputs_mr.shape[2]
    groups = channels // GROUP
    taps_se = kernel_se.shape[1]
    halo = 8

    wide = lax.all_gather(cotangent_out, "grp", axis=1, tiled=True)
    columns = lax.all_to_all(wide, "ctx", split_axis=1, concat_axis=0, tiled=True)
    term = lax.dot_general(
        columns, out_weight, (((1,), (1,)), ((), ())), preferred_element_type=F32
    ).astype(BF16)
    upstream = lax.psum_scatter(term, "ctx", scatter_dimension=0, tiled=True)

    before_mr = lax.ppermute(gated(inputs_mr[1], inputs_mr[2]), "ctx", up)
    before_se = lax.ppermute(
        gated(inputs_se[1, rows - halo :], inputs_se[2, rows - halo :]), "ctx", up
    )
    after_se = lax.ppermute(gated(cotangent_se[:halo], inputs_se[0, :halo]), "ctx", down)

    taps_f = kernel_mr.astype(F32)
    blank = jnp.zeros((groups, 1), F32)
    base_forward = jnp.concatenate(
        [blank, taps_f[:, ::-1], jnp.zeros((groups, rows - 1), F32)], 1
    )
    base_backward = jnp.concatenate([taps_f, jnp.zeros((groups, rows), F32)], 1)
    conv_mr, mixed_mr = mr_forward(inputs_mr, before_mr, base_forward, skip_mr[None])
    gathered = lax.all_gather(mixed_mr, "ctx", axis=0, tiled=True)

    filters = jnp.repeat(kernel_se.astype(F32).T, GROUP, axis=1)
    filters = jnp.concatenate([filters, jnp.zeros((halo - taps_se, channels), F32)], 0)
    mixed_se, grads_se, sums_se = se_operator(
        inputs_se, cotangent_se, before_se.astype(F32), after_se.astype(F32), filters,
        skip_se[None], taps_se,
    )

    after_mr = lax.ppermute(gated(upstream, inputs_mr[0]), "ctx", down)
    grads_mr, cross, skip_part_mr = mr_backward(
        inputs_mr, before_mr, upstream, after_mr, conv_mr, base_backward, skip_mr[None]
    )
    diagonals = cross[:, 0, 1 : rows + 1]
    for b in range(1, 8):
        diagonals = diagonals + cross[:, b, b + 1 : b + rows + 1]
    kernel_part_mr = diagonals[:, ::-1]
    kernel_part_se = sums_se.reshape(halo, groups, GROUP).sum(2).T
    packed = jnp.concatenate(
        [
            kernel_part_mr,
            kernel_part_se,
            sums_se[0].reshape(groups, GROUP),
            skip_part_mr.reshape(groups, GROUP),
        ],
        1,
    )
    packed = lax.psum(packed, "ctx")
    at = rows + halo
    grad_kernel_mr = packed[:, :rows]
    grad_kernel_se = packed[:, rows : rows + taps_se]
    grad_skip_se = packed[:, at : at + GROUP].reshape(channels)
    grad_skip_mr = packed[:, at + GROUP : at + 2 * GROUP].reshape(channels)

    partial_value = jnp.dot(gathered, out_weight, preferred_element_type=F32).astype(BF16)
    grad_out_weight = lax.dot_general(
        gathered, columns, (((0,), (0,)), ((), ())), preferred_element_type=F32
    )
    spread_value = lax.all_to_all(partial_value, "ctx", split_axis=0, concat_axis=1, tiled=True)
    projected = lax.psum_scatter(spread_value, "grp", scatter_dimension=1, tiled=True)
    return (
        mixed_se, projected, grads_se, grads_mr, grad_kernel_se, grad_kernel_mr, grad_skip_se,
        grad_skip_mr, grad_out_weight,
    )


def solution(mesh):
    placed = (
        P(None, "ctx", "grp"),
        P("ctx", "grp"),
        P("grp", None),
        P("grp"),
        P(None, "ctx", "grp"),
        P("grp", None),
        P("grp"),
        P("grp", "ctx"),
        P("ctx", "grp"),
    )
    return jax.shard_map(
        on_device,
        mesh=mesh,
        in_specs=placed,
        out_specs=(
            P("ctx", "grp"),
            P("ctx", "grp"),
            P(None, "ctx", "grp"),
            P(None, "ctx", "grp"),
            P("grp", None),
            P("grp", None),
            P("grp"),
            P("grp"),
            P("grp", "ctx"),
        ),
        check_vma=False,
    )
```

time: 1220 us -> 591 us (0.48); the launches traced: 1210 us -> 590 us
  blocking collectives: 191 us -> 30.6 us
  local copies, waits for them, and re-layouts: 181 us -> 26.1 us
  waiting for transfers between devices: 528 us -> 415 us
  starting transfers between devices: 117 us -> 22.3 us
  other arithmetic: 106 us -> 11.6 us
  Pallas kernels: 0 us -> 41.7 us
  matrix products: 67.3 us -> 28.2 us
    all_to_all x7 -> x1, waiting for transfers between devices: 264 us -> 0.01 us  [on_device(): lax.all_to_all(partial_value, 'ctx', split_axis=0, concat_axis=1, tiled=T...]
    all_gather x4 -> x0, blocking collectives: 159 us -> none  [the longest x1 83.9 us: on_device(): lax.all_gather(skip_part_se, 'ctx', axis=0, tiled=True)]
    reduce_scatter x2, waiting for transfers between devices: 0.01 us -> 151 us  [the longest x1 144 us: on_device(): upstream = lax.psum_scatter(term, 'ctx', scatter_dimension=0, tiled=True)]
    all_to_all x7 -> x1, starting transfers between devices: 117 us -> 4.47 us  [on_device(): lax.all_to_all(partial_value, 'ctx', split_axis=0, concat_axis=1, tiled=T...]
    all_gather x2, waiting for transfers between devices: 263 us -> 154 us  [the longest x1 129 us: on_device(): gathered = lax.all_gather(mixed_mr, 'ctx', axis=0, tiled=True)]
    psum x0 -> x1, waiting for transfers between devices: none -> 107 us  [on_device(): packed = lax.psum(packed, 'ctx')]
    unnamed x4 -> x0, other arithmetic: 66.2 us -> none
    convert_element_type x10 -> x0, local copies, waits for them, and re-layouts: 45.8 us -> none  [the longest x4 28 us: forward(): mixed = (inputs[0] * convolved).astype(jnp.bfloat16)]
  transfers between devices with their start and end apart: 11 -> 10, of which waited for: 7 -> 7; matrix products, arithmetic and copies ran while one was open for 22% -> 7% of each run, Pallas kernels for 0% -> 7%
where the time goes in v1:
time: 591 us; the launch traced here: 590 us
  waiting for transfers between devices  415 us (70%)
  Pallas kernels  41.7 us (7%)
  blocking collectives  30.6 us (5%)
  matrix products  28.2 us (5%)
  local copies, waits for them, and re-layouts  26.1 us (4%)
  starting transfers between devices  22.3 us (4%)
  between operations  14.1 us (2%)
  other arithmetic  11.6 us (2%)
    reduce_scatter x1, waiting for transfers between devices, on_device(): upstream = lax.psum_scatter(term, 'ctx', scatter_dimension=0, tiled=True)  144 us
    all_gather x1, waiting for transfers between devices, on_device(): gathered = lax.all_gather(mixed_mr, 'ctx', axis=0, tiled=True)  129 us
    psum x1, waiting for transfers between devices, on_device(): packed = lax.psum(packed, 'ctx')  107 us
    all_to_all x1, blocking collectives, on_device(): lax.all_to_all(wide, 'ctx', split_axis=1, concat_axis=0, tiled=True)  30.6 us
    all_gather x1, waiting for transfers between devices, on_device(): wide = lax.all_gather(cotangent_out, 'grp', axis=1, tiled=True)  24.7 us
    pallas_call x1, Pallas kernels, mr_backward(): pl.pallas_call(mr_backward_kernel, grid=(channels // LANES,), in_specs=[c...  21.9 us
    unnamed x36, local copies, waits for them, and re-layouts  14.8 us
    ppermute x1, starting transfers between devices, on_device(): lax.ppermute(gated(inputs_se[1, rows - halo:], inputs_se[2, rows - halo:]...  12 us
  transfers between devices with their start and end apart: 10, of which 7 were waited for; matrix products, arithmetic and copies ran while one was open for 7% of the time, Pallas kernels for 7%

profile of v1, /device:TPU:0, one launch (start us, length us, event | category | flops | bytes accessed | tf_op | source)
XLA Modules:
  0.0 589.9 jit_solution(4220627905967545550)
XLA Ops:
  7.2 2.2 copy.27
  9.5 24.7 %all-gather.5.cloned.1.call-done = bf16[128,4096]{0,1:T(8,128)(2,1)} async-done(((bf16[128,2048]{0,1:T(8,128)(2,1)}), bf16[128,4096]{0,1:T(8,128)(2,1)}) %all-gather.5.cloned.1.call-update) | async-done | bytes 1048592 | tf_op jit(solution)/shard_map/all_gather | solution.py:203
  34.2 30.6 %all_to_all.38 = bf16[128,16,256]{0,2,1:T(8,128)(2,1)} all-to-all(bf16[128,16,256]{0,2,1:T(8,128)(2,1)} %bitcast.38), channel_id=1, replica_groups=mesh['ctx'=16,'grp'=2] {'ctx'}, dimensions={1} | all-to-all | bytes 2097152 | tf_op jit(solution)/shard_map/all_to_all | solution.py:204
  66.3 8.3 %convolution_convert_fusion = bf16[2048,4096]{1,0:T(8,128)(2,1)} fusion(bf16[2048,256]{1,0:T(8,128)(2,1)S(1)} %bitcast.33, bf16[4096,256]{1,0:T(8,128)(2,1)S(1)} %copy-done), kind=kOutput, calls=%fused_computation | convolution fusion | flops 4303355904 | bytes 19922944 | tf_op jit(solution)/shard_map/dot_general | solution.py:205
  74.6 2.8 fusion.1
  77.4 2.7 collective-permute-start.2
  80.5 2.0 collective-permute-done.2.before_ref
  82.6 2.8 copy-done.3
  85.4 9.9 %mr_forward.1 = (f32[128,4096]{1,0:T(8,128)S(1)}, bf16[128,4096]{1,0:T(8,128)(2,1)}) custom-call(bf16[3,128,4096]{2,1,0:T(8,128)(2,1)S(1)} %copy-done.3, bf16[128,4096]{1,0:T(8,128)(2,1)S(1)} %collective-permute-done.2.before_ref, f32[256,256]{1,0:T(8,128)S(1)} %maximum_maximum_fusion.base_ref, f32[1,4096]{1,0:T(1,128)S(1)} %bitcast.31), custom_call_target="tpu_custom_call" | custom-call | flops 4294967296 | bytes 5767168 | tf_op jit(solution)/shard_map/mr_forward/pallas_call | solution.py:40
  97.6 12.0 %collective-permute-start = (bf16[8,4096]{1,0:T(8,128)(2,1)S(1)}, bf16[8,4096]{1,0:T(8,128)(2,1)S(1)}, u32[]{:S(2)}, u32[]{:S(2)}) collective-permute-start(bf16[8,4096]{1,0:T(8,128)(2,1)S(1)} %fusion.3), channel_id=1, source_target_pairs={{0,2},{2,4},{4,6},{6,8},{8,10},{10,12},{12,14},{14,16},{16,18},{18... | collective-permute-start | bytes 196616 | tf_op jit(solution)/shard_map/ppermute | solution.py:211
  109.6 144.1 %reduce-scatter.5.cloned.1.call-done.upstream_ref = bf16[128,4096]{1,0:T(8,128)(2,1)} async-done(((bf16[2048,4096]{1,0:T(8,128)(2,1)}), bf16[128,4096]{1,0:T(8,128)(2,1)}) %reduce-scatter.5.cloned.1.call-update) | async-done | bytes 1048592 | tf_op jit(solution)/shard_map/reduce_scatter | solution.py:208
  253.7 2.8 fusion
  257.9 129.4 %all-gather.3.cloned.1.call-done = bf16[2048,4096]{1,0:T(8,128)(2,1)} async-done(((bf16[128,4096]{1,0:T(8,128)(2,1)}), bf16[2048,4096]{1,0:T(8,128)(2,1)}) %all-gather.3.cloned.1.call-update) | async-done | bytes 16777232 | tf_op jit(solution)/shard_map/all_gather | solution.py:223
  387.3 9.2 %convolution_convert_fusion.1 = bf16[2048,256]{1,0:T(8,128)(2,1)} fusion(bf16[2048,4096]{1,0:T(8,128)(2,1)} %all-gather.3.cloned.1.call-done, bf16[4096,256]{1,0:T(8,128)(2,1)S(1)} %copy-done), kind=kOutput, calls=%fused_computation.1 | convolution fusion | flops 4295491584 | bytes 19922944 | tf_op jit(solution)/shard_map/dot_general | solution.py:257
  396.5 4.5 all-to-all-start
  405.1 1.9 copy-done.2
  407.0 9.8 %se_operator.1 = (bf16[128,4096]{1,0:T(8,128)(2,1)}, bf16[3,128,4096]{2,1,0:T(8,128)(2,1)}, f32[8,4096]{1,0:T(8,128)S(1)}) custom-call(bf16[3,128,4096]{2,1,0:T(8,128)(2,1)S(1)} %copy-done.2, bf16[128,4096]{1,0:T(8,128)(2,1)S(1)} %copy-done.5, f32[8,4096]{1,0:T(8,128)S(1)} %convert_element_type.72.refs_2_, f32[8,4096]{1,0:T(8,128)S(1)} %convert_element_type.77.refs_3_, ...), custom_call_target="tpu_custom_call" | custom-call | flops 26214400 | bytes 8388608 | tf_op jit(solution)/shard_map/se_operator/pallas_call | solution.py:168
  417.8 1.9 copy-done.4
  423.7 21.9 %mr_backward.1 = (bf16[3,128,4096]{2,1,0:T(8,128)(2,1)}, f32[256,8,256]{2,1,0:T(8,128)S(1)}, f32[1,4096]{1,0:T(1,128)S(1)}) custom-call(bf16[3,128,4096]{2,1,0:T(8,128)(2,1)S(1)} %copy-done.4, bf16[128,4096]{1,0:T(8,128)(2,1)S(1)} %copy-done.9, bf16[128,4096]{1,0:T(8,128)(2,1)S(1)} %copy-done.6, bf16[128,4096]{1,0:T(8,128)(2,1)} %collective-permute-done.3.after_ref, ...), custom_call_target="tpu_custom_call" | custom-call | flops 8589934592 | bytes 12582912 | tf_op jit(solution)/shard_map/mr_backward/pallas_call | solution.py:99
  445.7 2.2 add_add_fusion
  450.3 2.3 copy.31
  452.7 107.2 %all-reduce.4.cloned.1.call-done = f32[256,168]{1,0:T(8,128)} async-done(((f32[256,168]{1,0:T(8,128)}), f32[256,168]{1,0:T(8,128)}) %all-reduce.4.cloned.1.call-update) | async-done | bytes 172048 | tf_op jit(solution)/shard_map/psum | solution.py:250
  565.6 10.7 %fusion.5 = f32[4096,256]{1,0:T(8,128)} fusion(bf16[2048,4096]{1,0:T(8,128)(2,1)} %all-gather.3.cloned.1.call-done, bf16[2048,256]{1,0:T(8,128)(2,1)S(1)} %bitcast.34), kind=kOutput, calls=%fused_computation.16 | convolution fusion | flops 4294967296 | bytes 22020096 | tf_op jit(solution)/shard_map/dot_general | solution.py:258
  576.3 7.1 %reduce-scatter.3.cloned.1.call-done = bf16[128,2048]{1,0:T(8,128)(2,1)} async-done(((bf16[128,4096]{1,0:T(8,128)(2,1)}), bf16[128,2048]{1,0:T(8,128)(2,1)}) %reduce-scatter.3.cloned.1.call-update) | async-done | bytes 524304 | tf_op jit(solution)/shard_map/reduce_scatter | solution.py:262
  (78 shorter events, 22.8 us)
Async XLA Ops:
  7.2 59.1 %copy-start = (bf16[4096,256]{1,0:T(8,128)(2,1)S(1)}, bf16[4096,256]{1,0:T(8,128)(2,1)}, u32[]{:S(2)}) copy-start(bf16[4096,256]{1,0:T(8,128)(2,1)} %param.16) | copy-start | bytes 6291460
  7.2 27.0 %all-gather.5.cloned.1.call-start = ((), (), s32[]{:S(2)}) async-start(), calls=%async_computation.6 | async-start | bytes 1572864 | tf_op jit(solution)/shard_map/all_gather | solution.py:203
  9.4 244.3 %reduce-scatter.5.cloned.1.call-start = ((), (), s32[]{:S(2)}) async-start(), calls=%async_computation.7 | async-start | bytes 17825792 | tf_op jit(solution)/shard_map/reduce_scatter | solution.py:208
  66.2 8.3 %copy-start.13 = (bf16[16,128,256]{2,1,0:T(8,128)(2,1)}, bf16[16,128,256]{2,1,0:T(8,128)(2,1)S(1)}, u32[]{:S(2)}) copy-start(bf16[16,128,256]{2,1,0:T(8,128)(2,1)S(1)} %copy.28) | copy-start | bytes 3145732
  74.6 5.6 copy-start.15
  74.6 8.0 %copy-start.10 = (f32[4096]{0:T(1024)S(1)}, f32[4096]{0:T(1024)}, u32[]{:S(2)}) copy-start(f32[4096]{0:T(1024)} %param.15) | copy-start | bytes 49156
  74.6 312.7 %all-gather.3.cloned.1.call-start = ((), (), s32[]{:S(2)}) async-start(), calls=%async_computation.4 | async-start | bytes 17825792 | tf_op jit(solution)/shard_map/all_gather | solution.py:223
  77.4 5.2 collective-permute-start.2
  82.6 12.8 %copy-start.8 = (bf16[128,4096]{1,0:T(8,128)(2,1)}, bf16[128,4096]{1,0:T(8,128)(2,1)S(1)}, u32[]{:S(2)}) copy-start(bf16[128,4096]{1,0:T(8,128)(2,1)S(1)} %collective-permute-done.2.before_ref) | copy-start | bytes 3145732
  82.6 2.8 copy-start.3
  97.6 306.6 %collective-permute-start = (bf16[8,4096]{1,0:T(8,128)(2,1)S(1)}, bf16[8,4096]{1,0:T(8,128)(2,1)S(1)}, u32[]{:S(2)}, u32[]{:S(2)}) collective-permute-start(bf16[8,4096]{1,0:T(8,128)(2,1)S(1)} %fusion.3), channel_id=1, source_target_pairs={{0,2},{2,4},{4,6},{6,8},{8,10},{10,12},{12,14},{14,16},{16,18},{18... | collective-permute-start | bytes 196616 | tf_op jit(solution)/shard_map/ppermute | solution.py:211
  256.5 144.5 %copy-start.5 = (bf16[128,4096]{1,0:T(8,128)(2,1)S(1)}, bf16[128,4096]{1,0:T(8,128)(2,1)}, u32[]{:S(2)}) copy-start(bf16[128,4096]{1,0:T(8,128)(2,1)} %refs_1_.1) | copy-start | bytes 3145732
  256.5 146.9 %copy-start.16 = (bf16[256,7]{0,1:T(8,128)(2,1)S(1)}, bf16[256,7]{0,1:T(8,128)(2,1)}, u32[]{:S(2)}) copy-start(bf16[256,7]{0,1:T(8,128)(2,1)} %param.11) | copy-start | bytes 10756
  256.5 161.3 %collective-permute-start.3 = (bf16[128,4096]{1,0:T(8,128)(2,1)}, bf16[128,4096]{1,0:T(8,128)(2,1)}, u32[]{:S(2)}, u32[]{:S(2)}) collective-permute-start(bf16[128,4096]{1,0:T(8,128)(2,1)} %fusion), channel_id=1, source_target_pairs={{2,0},{4,2},{6,4},{8,6},{10,8},{12,10},{14,12},{16,14},{18,16},{20... | collective-permute-start | bytes 3145736 | tf_op jit(solution)/shard_map/ppermute | solution.py:232
  396.5 8.6 %copy-start.7 = (f32[4096]{0:T(1024)S(1)}, f32[4096]{0:T(1024)}, u32[]{:S(2)}) copy-start(f32[4096]{0:T(1024)} %param.12) | copy-start | bytes 49156
  396.5 53.8 %all-to-all-start = ((bf16[16,128,256]{2,1,0:T(8,128)(2,1)}), bf16[16,128,256]{2,1,0:T(8,128)(2,1)}, u32[]{:S(2)}, u32[]{:S(2)}) async-start(bf16[16,128,256]{2,1,0:T(8,128)(2,1)} %bitcast.37), calls=%async_computation | async-start | bytes 2097152 | tf_op jit(solution)/shard_map/all_to_all | solution.py:261
  401.0 158.9 %all-reduce.4.cloned.1.call-start = ((), (), s32[]{:S(2)}) async-start(), calls=%async_computation.8 | async-start | bytes 524288 | tf_op jit(solution)/shard_map/psum | solution.py:250
  401.9 3.1 collective-permute-start.1
  405.1 1.9 copy-start.2
  417.8 1.9 copy-start.4
  422.1 1.6 copy-start.12
  447.9 117.7 %copy-start.14 = (bf16[16,128,256]{2,1,0:T(8,128)(2,1)S(1)}, bf16[16,128,256]{2,1,0:T(8,128)(2,1)}, u32[]{:S(2)}) copy-start(bf16[16,128,256]{2,1,0:T(8,128)(2,1)} %copy-done.13) | copy-start | bytes 3145732
  450.3 133.1 %reduce-scatter.3.cloned.1.call-start = ((), (), s32[]{:S(2)}) async-start(), calls=%async_computation.5 | async-start | bytes 1572864 | tf_op jit(solution)/shard_map/reduce_scatter | solution.py:262
  565.6 17.8 %copy-start.1 = (bf16[4096,256]{1,0:T(8,128)(2,1)S(1)}, bf16[4096,256]{1,0:T(8,128)(2,1)}, u32[]{:S(2)}) copy-start(bf16[4096,256]{1,0:T(8,128)(2,1)} %param.16) | copy-start | bytes 6291460
  (3 other events, 3.8 us)
Sparse Core Ops, SparseCore 0:
  10.1 23.9 all-gather.4
  74.7 179.0 reduce-scatter.4
  256.5 130.8 all-gather.2
  450.4 109.4 all-reduce.3
  562.5 20.8 reduce-scatter.2

commit v2 on v1

--- a/solution.py
+++ b/solution.py
@@ -183,6 +183,281 @@
     )(inputs, cotangent, before, after, filters, skip)
 
 
+MESH = pl.DeviceIdType.MESH
+
+
+def greet_all(n, m, me, mine):
+    barrier = pltpu.get_barrier_semaphore()
+
+    def one(k, carry):
+        there = lax.rem(me * m + mine + k, n * m)
+        pl.semaphore_signal(
+            barrier, inc=1, device_id=(there // m, lax.rem(there, m)), device_id_type=MESH
+        )
+        return carry
+
+    lax.fori_loop(1, n * m, one, 0)
+    pl.semaphore_wait(barrier, n * m - 1)
+
+
+def ring_kernel(
+    n, m, tile, cot_ref, weight_ref, out_ref, columns_ref, cols, sib, weight_sib, sums, outgoing,
+    incoming, cot_send, cot_recv, local_sem, pair_send, pair_recv, ring_send, ring_recv,
+):
+    me, mine = lax.axis_index("ctx"), lax.axis_index("grp")
+    rows = cot_ref.shape[0]
+    channels, width = weight_ref.shape
+    per = cot_ref.shape[1] // width
+    half, hops = rows // 2, n // 2
+    core, chip = lax.rem(me, 2), me // 2
+    sibling = me + 1 - 2 * core
+    depth = hops // 2
+
+    def chip_at(place):
+        turn = place // depth
+        z = (1 - turn) * place + turn * (2 * depth - 1 - place)
+        return 2 * z + turn
+
+    x, z = lax.rem(chip, 2), chip // 2
+    place = (1 - x) * z + x * (2 * depth - 1 - z)
+    right = 2 * chip_at(lax.rem(place + 1, hops)) + core
+    left = 2 * chip_at(lax.rem(place + hops - 1, hops)) + core
+    greet_all(n, m, me, mine)
+
+    def pair_copy(source, target, k):
+        return pltpu.make_async_remote_copy(
+            src_ref=source, dst_ref=target, send_sem=pair_send.at[k], recv_sem=pair_recv.at[k],
+            device_id=(sibling, mine), device_id_type=MESH,
+        )
+
+    weight_copy = pair_copy(weight_ref, weight_sib, 0)
+    weight_copy.start()
+
+    def cot_copy(b, g, source):
+        return pltpu.make_async_remote_copy(
+            src_ref=cot_ref.at[:, b * width : (b + 1) * width],
+            dst_ref=cols.at[lax.rem(source, 2), source // 2],
+            send_sem=cot_send.at[b, g], recv_sem=cot_recv.at[source],
+            device_id=(mine * per + b, g), device_id_type=MESH,
+        )
+
+    for b in range(per):
+        for g in range(m):
+            own = jnp.logical_and(mine * per + b == me, mine == g)
+
+            @pl.when(jnp.logical_not(own))
+            def _(b=b, g=g):
+                cot_copy(b, g, me).start()
+
+            @pl.when(own)
+            def _(b=b):
+                copy = pltpu.make_async_copy(
+                    cot_ref.at[:, b * width : (b + 1) * width], cols.at[core, chip], local_sem
+                )
+                copy.start()
+                copy.wait()
+
+    def arrive(source, carry):
+        own = jnp.logical_and(source == me, me // per == mine)
+
+        @pl.when(jnp.logical_not(own))
+        def _():
+            cot_copy(0, 0, source).wait_recv()
+
+        return carry
+
+    lax.fori_loop(0, n, arrive, 0)
+    cols_copy = pair_copy(cols.at[1 - core], sib, 1)
+    cols_copy.start()
+    columns_ref[...] = cols[...]
+    weight_copy.wait_recv()
+    cols_copy.wait_recv()
+
+    def terms(owners):
+        def one(t, carry):
+            at = pl.ds(pl.multiple_of(t * tile, tile), tile)
+            for d in range(2):
+                part = pl.ds(d * half, half)
+                dims = (((1,), (1,)), ((), ()))
+                near = lax.dot_general(
+                    cols[core, owners[d], part, :], weight_ref[at, :], dims,
+                    preferred_element_type=F32,
+                )
+                far = lax.dot_general(
+                    sib[owners[d], part, :], weight_sib[at, :], dims, preferred_element_type=F32
+                )
+                sums[d, :, at] = near + far
+            return carry
+
+        lax.fori_loop(0, channels // tile, one, 0)
+
+    def hop(d, s):
+        return pltpu.make_async_remote_copy(
+            src_ref=outgoing.at[d, s], dst_ref=incoming.at[d, s],
+            send_sem=ring_send.at[d, s], recv_sem=ring_recv.at[d, s],
+            device_id=((right, left)[d], mine), device_id_type=MESH,
+        )
+
+    def owners_at(s):
+        return (
+            chip_at(lax.rem(place + 2 * hops - 1 - s, hops)),
+            chip_at(lax.rem(place + 1 + s, hops)),
+        )
+
+    terms(owners_at(0))
+    for d in range(2):
+        outgoing[d, 0] = sums[d].astype(BF16)
+        hop(d, 0).start()
+
+    def step(s, carry):
+        terms(owners_at(s))
+        for d in range(2):
+            hop(d, s - 1).wait_recv()
+            outgoing[d, s] = (sums[d] + incoming[d, s - 1].astype(F32)).astype(BF16)
+            hop(d, s).start()
+        return carry
+
+    lax.fori_loop(1, hops - 1, step, 0)
+    terms((chip, chip))
+    for d in range(2):
+        hop(d, hops - 2).wait_recv()
+        out_ref[d * half : (d + 1) * half] = (
+            sums[d] + incoming[d, hops - 2].astype(F32)
+        ).astype(BF16)
+
+    def sent(s, carry):
+        for d in range(2):
+            hop(d, s).wait_send()
+        return carry
+
+    lax.fori_loop(0, hops - 1, sent, 0)
+    weight_copy.wait_send()
+    cols_copy.wait_send()
+    for b in range(per):
+        for g in range(m):
+            own = jnp.logical_and(mine * per + b == me, mine == g)
+
+            @pl.when(jnp.logical_not(own))
+            def _(b=b, g=g):
+                cot_copy(b, g, me).wait_send()
+
+
+def ring_upstream(cotangent, weight):
+    n, m = lax.axis_size("ctx"), lax.axis_size("grp")
+    rows = cotangent.shape[0]
+    channels, width = weight.shape
+    hops, half = n // 2, rows // 2
+    tile = min(512, channels)
+    dma = pltpu.SemaphoreType.DMA
+
+    def kernel(*refs):
+        ring_kernel(n, m, tile, *refs)
+
+    vmem = pl.BlockSpec(memory_space=pltpu.VMEM)
+    upstream, columns = pl.pallas_call(
+        kernel,
+        in_specs=[vmem, vmem],
+        out_specs=[vmem, vmem],
+        out_shape=[
+            jax.ShapeDtypeStruct((rows, channels), BF16),
+            jax.ShapeDtypeStruct((2, hops, rows, width), BF16),
+        ],
+        scratch_shapes=[
+            pltpu.VMEM((2, hops, rows, width), BF16),
+            pltpu.VMEM((hops, rows, width), BF16),
+            pltpu.VMEM((channels, width), BF16),
+            pltpu.VMEM((2, half, channels), F32),
+            pltpu.VMEM((2, hops - 1, half, channels), BF16),
+            pltpu.VMEM((2, hops - 1, half, channels), BF16),
+            dma((cotangent.shape[1] // width, m)), dma((n,)), dma,
+            dma((2,)), dma((2,)), dma((2, hops - 1)), dma((2, hops - 1)),
+        ],
+        compiler_params=pltpu.CompilerParams(
+            collective_id=0, has_side_effects=True, vmem_limit_bytes=44 * 2**20
+        ),
+        cost_estimate=pl.CostEstimate(
+            flops=2 * n * rows * channels * width, bytes_accessed=300 * 2**20, transcendentals=0
+        ),
+        name="ring_upstream",
+    )(cotangent, weight)
+    return upstream, jnp.swapaxes(columns, 0, 1).reshape(n * rows, width)
+
+
+def sum_kernel(n, m, part_ref, total_ref, landed, shared, first_send, first_recv, last_send, last_recv):
+    me, mine = lax.axis_index("ctx"), lax.axis_index("grp")
+    barrier = pltpu.get_barrier_semaphore()
+
+    def greet(k, carry):
+        pl.semaphore_signal(
+            barrier, inc=1, device_id=(lax.rem(me + k, n), mine), device_id_type=MESH
+        )
+        return carry
+
+    lax.fori_loop(1, n, greet, 0)
+    pl.semaphore_wait(barrier, n - 1)
+
+    def first(k, source):
+        there = lax.rem(me + k, n)
+        return pltpu.make_async_remote_copy(
+            src_ref=part_ref.at[there], dst_ref=landed.at[source], send_sem=first_send.at[k],
+            recv_sem=first_recv.at[source], device_id=(there, mine), device_id_type=MESH,
+        )
+
+    def last(k, source):
+        there = lax.rem(me + k, n)
+        return pltpu.make_async_remote_copy(
+            src_ref=shared.at[me], dst_ref=shared.at[source], send_sem=last_send.at[k],
+            recv_sem=last_recv.at[source], device_id=(there, mine), device_id_type=MESH,
+        )
+
+    def loop(body):
+        def one(k, carry):
+            body(k)
+            return carry
+
+        lax.fori_loop(1, n, one, 0)
+
+    loop(lambda k: first(k, me).start())
+
+    def add(k, total):
+        source = lax.rem(me + k, n)
+        first(k, source).wait_recv()
+        return total + landed[source]
+
+    shared[me] = lax.fori_loop(1, n, add, part_ref[me])
+    loop(lambda k: last(k, me).start())
+    loop(lambda k: last(k, lax.rem(me + k, n)).wait_recv())
+    total_ref[...] = shared[...]
+    loop(lambda k: first(k, me).wait_send())
+    loop(lambda k: last(k, me).wait_send())
+
+
+def sum_over_ctx(part):
+    n, m = lax.axis_size("ctx"), lax.axis_size("grp")
+    shape = (n, part.shape[0] // n, part.shape[1])
+    dma = pltpu.SemaphoreType.DMA
+
+    def kernel(*refs):
+        sum_kernel(n, m, *refs)
+
+    vmem = pl.BlockSpec(memory_space=pltpu.VMEM)
+    total = pl.pallas_call(
+        kernel,
+        in_specs=[vmem],
+        out_specs=vmem,
+        out_shape=jax.ShapeDtypeStruct(shape, F32),
+        scratch_shapes=[pltpu.VMEM(shape, F32), pltpu.VMEM(shape, F32)] + [dma((n,))] * 4,
+        compiler_params=pltpu.CompilerParams(
+            collective_id=1, has_side_effects=True, vmem_limit_bytes=16 * 2**20
+        ),
+        cost_estimate=pl.CostEstimate(
+            flops=part.size, bytes_accessed=40 * 2**20, transcendentals=0
+        ),
+        name="sum_over_ctx",
+    )(part.reshape(shape))
+    return total.reshape(part.shape)
+
+
 def gated(left, right):
     return (left.astype(F32) * right.astype(F32)).astype(BF16)
 
@@ -200,13 +475,6 @@
     taps_se = kernel_se.shape[1]
     halo = 8
 
-    wide = lax.all_gather(cotangent_out, "grp", axis=1, tiled=True)
-    columns = lax.all_to_all(wide, "ctx", split_axis=1, concat_axis=0, tiled=True)
-    term = lax.dot_general(
-        columns, out_weight, (((1,), (1,)), ((), ())), preferred_element_type=F32
-    ).astype(BF16)
-    upstream = lax.psum_scatter(term, "ctx", scatter_dimension=0, tiled=True)
-
     before_mr = lax.ppermute(gated(inputs_mr[1], inputs_mr[2]), "ctx", up)
     before_se = lax.ppermute(
         gated(inputs_se[1, rows - halo :], inputs_se[2, rows - halo :]), "ctx", up
@@ -220,6 +488,8 @@
     )
     base_backward = jnp.concatenate([taps_f, jnp.zeros((groups, rows), F32)], 1)
     conv_mr, mixed_mr = mr_forward(inputs_mr, before_mr, base_forward, skip_mr[None])
+    upstream, columns = ring_upstream(cotangent_out, out_weight)
+    mixed_mr, upstream = lax.optimization_barrier((mixed_mr, upstream))
     gathered = lax.all_gather(mixed_mr, "ctx", axis=0, tiled=True)
 
     filters = jnp.repeat(kernel_se.astype(F32).T, GROUP, axis=1)
@@ -244,10 +514,12 @@
             kernel_part_se,
             sums_se[0].reshape(groups, GROUP),
             skip_part_mr.reshape(groups, GROUP),
+            jnp.zeros((groups, -(rows + halo + 2 * GROUP) % 128), F32),
         ],
         1,
     )
-    packed = lax.psum(packed, "ctx")
+    packed = sum_over_ctx(packed)
+    packed, gathered = lax.optimization_barrier((packed, gathered))
     at = rows + halo
     grad_kernel_mr = packed[:, :rows]
     grad_kernel_se = packed[:, rows : rows + taps_se]

time: 591 us -> 393 us (0.66)
  waiting for transfers between devices: 415 us -> 28.5 us
  Pallas kernels: 41.7 us -> 259 us
  starting transfers between devices: 22.3 us -> 7.26 us
  matrix products: 28.2 us -> 18.8 us
    pallas_call x0 -> x2, Pallas kernels: none -> 218 us  [the longest x1 149 us: ring_upstream(): pl.pallas_call(kernel, in_specs=[vmem, vmem], out_specs=[vmem, vmem], out...]
    reduce_scatter x1 -> x0, waiting for transfers between devices: 144 us -> none  [on_device(): upstream = lax.psum_scatter(term, 'ctx', scatter_dimension=0, tiled=True)]
    all_gather x1, waiting for transfers between devices: 129 us -> 21.3 us  [on_device(): gathered = lax.all_gather(mixed_mr, 'ctx', axis=0, tiled=True)]
    psum x1 -> x0, waiting for transfers between devices: 107 us -> none  [on_device(): packed = lax.psum(packed, 'ctx')]
    all_gather x1 -> x0, waiting for transfers between devices: 24.7 us -> none  [on_device(): wide = lax.all_gather(cotangent_out, 'grp', axis=1, tiled=True)]
    ppermute x1, starting transfers between devices: 12 us -> 2.03 us  [on_device(): lax.ppermute(gated(inputs_se[1, rows - halo:], inputs_se[2, rows - halo:]...]
    dot_general x1 -> x0, matrix products: 8.26 us -> none  [on_device(): lax.dot_general(columns, out_weight, (((1,), (1,)), ((), ())), preferred_...]
    unnamed x36 -> x45, local copies, waits for them, and re-layouts: 14.8 us -> 14.2 us
  transfers between devices with their start and end apart: 10 -> 6, of which waited for: 7 -> 2; matrix products, arithmetic and copies ran while one was open for 7% -> 7% of each run, Pallas kernels for 7% -> 64%
where the time goes in v2:
time: 393 us; the launch traced here: 392 us
  Pallas kernels  259 us (66%)
  waiting for transfers between devices  28.5 us (7%)
  blocking collectives  28.5 us (7%)
  local copies, waits for them, and re-layouts  22.4 us (6%)
  matrix products  18.8 us (5%)
  between operations  14.4 us (4%)
  other arithmetic  12.9 us (3%)
  starting transfers between devices  7.26 us (2%)
    pallas_call x1, Pallas kernels, ring_upstream(): pl.pallas_call(kernel, in_specs=[vmem, vmem], out_specs=[vmem, vmem], out...  149 us
    pallas_call x1, Pallas kernels, sum_over_ctx(): pl.pallas_call(kernel, in_specs=[vmem], out_specs=vmem, out_shape=jax.Sha...  69 us
    all_to_all x1, blocking collectives, on_device(): lax.all_to_all(partial_value, 'ctx', split_axis=0, concat_axis=1, tiled=T...  28.5 us
    pallas_call x1, Pallas kernels, mr_backward(): pl.pallas_call(mr_backward_kernel, grid=(channels // LANES,), in_specs=[c...  21.9 us
    all_gather x1, waiting for transfers between devices, on_device(): gathered = lax.all_gather(mixed_mr, 'ctx', axis=0, tiled=True)  21.3 us
    unnamed x45, local copies, waits for them, and re-layouts  14.2 us
    dot_general x1, matrix products, on_device(): lax.dot_general(gathered, columns, (((0,), (0,)), ((), ())), preferred_el...  10.6 us
    pallas_call x1, Pallas kernels, se_operator(): pl.pallas_call(kernel, grid=(channels // LANES,), in_specs=[cube, flat, e...  9.82 us
  transfers between devices with their start and end apart: 6, of which 2 were waited for; matrix products, arithmetic and copies ran while one was open for 7% of the time, Pallas kernels for 64%

profile of v2, /device:TPU:0, one launch (start us, length us, event | category | flops | bytes accessed | tf_op | source)
XLA Modules:
  0.0 391.8 jit_solution(8472631419252925113)
XLA Ops:
  7.2 2.9 fusion.1
  10.2 2.4 collective-permute-start.2
  14.0 149.3 %ring_upstream.1 = (bf16[128,4096]{1,0:T(8,128)(2,1)S(1)}, bf16[2,8,128,256]{3,2,1,0:T(8,128)(2,1)S(1)}) custom-call(bf16[128,2048]{1,0:T(8,128)(2,1)S(1)} %copy-done.15, bf16[4096,256]{1,0:T(8,128)(2,1)S(1)} %copy-done.10), custom_call_target="tpu_custom_call" | custom-call | flops 4294967296 | bytes 314572800 | tf_op jit(solution)/shard_map/ring_upstream/pallas_call | solution.py:357
  164.4 1.2 copy-done.13
  165.6 8.9 %mr_forward.1 = (f32[128,4096]{1,0:T(8,128)S(1)}, bf16[128,4096]{1,0:T(8,128)(2,1)S(1)}) custom-call(bf16[3,128,4096]{2,1,0:T(8,128)(2,1)S(1)} %copy-done.1, bf16[128,4096]{1,0:T(8,128)(2,1)S(1)} %copy-done.13, f32[256,256]{1,0:T(8,128)S(1)} %maximum_maximum_fusion.base_ref, f32[1,4096]{1,0:T(1,128)S(1)} %bitcast.35), custom_call_target="tpu_custom_call" | custom-call | flops 4294967296 | bytes 5767168 | tf_op jit(solution)/shard_map/mr_forward/pallas_call | solution.py:40
  175.5 1.3 copy-done.18
  177.5 2.0 collective-permute-start
  179.6 2.8 fusion
  182.4 1.3 collective-permute-start.3
  183.7 1.5 fusion.2
  185.1 1.5 collective-permute-start.1
  186.7 1.2 broadcast_in_dim.21
  187.9 1.7 reshape.64
  192.6 9.8 %se_operator.1 = (bf16[128,4096]{1,0:T(8,128)(2,1)}, bf16[3,128,4096]{2,1,0:T(8,128)(2,1)}, f32[8,4096]{1,0:T(8,128)S(1)}) custom-call(bf16[3,128,4096]{2,1,0:T(8,128)(2,1)S(1)} %copy-done, bf16[128,4096]{1,0:T(8,128)(2,1)S(1)} %copy-done.3, f32[8,4096]{1,0:T(8,128)S(1)} %convert_element_type.69.refs_2_, f32[8,4096]{1,0:T(8,128)S(1)} %convert_element_type.74.refs_3_, ...), custom_call_target="tpu_custom_call" | custom-call | flops 26214400 | bytes 8388608 | tf_op jit(solution)/shard_map/se_operator/pallas_call | solution.py:168
  203.5 1.9 copy-done.2
  208.5 1.6 copy-done.19
  210.1 21.9 %mr_backward.1 = (bf16[3,128,4096]{2,1,0:T(8,128)(2,1)}, f32[256,8,256]{2,1,0:T(8,128)S(1)}, f32[1,4096]{1,0:T(1,128)S(1)}) custom-call(bf16[3,128,4096]{2,1,0:T(8,128)(2,1)S(1)} %copy-done.2, bf16[128,4096]{1,0:T(8,128)(2,1)S(1)} %copy-done.14, bf16[128,4096]{1,0:T(8,128)(2,1)S(1)} %copy-done.5, bf16[128,4096]{1,0:T(8,128)(2,1)} %collective-permute-done.3.after_ref, ...), custom_call_target="tpu_custom_call" | custom-call | flops 8589934592 | bytes 12582912 | tf_op jit(solution)/shard_map/mr_backward/pallas_call | solution.py:99
  232.1 2.2 add_add_fusion
  236.0 69.0 %sum_over_ctx.1 = f32[16,16,256]{2,1,0:T(8,128)S(1)} custom-call(f32[16,16,256]{2,1,0:T(8,128)S(1)} %concatenate.28.refs_0_), custom_call_target="tpu_custom_call" | custom-call | flops 65536 | bytes 41943040 | tf_op jit(solution)/shard_map/sum_over_ctx/pallas_call | solution.py:444
  305.1 21.3 %all-gather.2.cloned.1.call-done = bf16[2048,4096]{1,0:T(8,128)(2,1)} async-done(((bf16[128,4096]{1,0:T(8,128)(2,1)}), bf16[2048,4096]{1,0:T(8,128)(2,1)}) %all-gather.2.cloned.1.call-update) | async-done | bytes 16777232 | tf_op jit(solution)/shard_map/all_gather | solution.py:493
  326.3 8.2 %convolution_convert_fusion = bf16[2048,256]{1,0:T(8,128)(2,1)S(1)} fusion(bf16[2048,4096]{1,0:T(8,128)(2,1)} %all-gather.2.cloned.1.call-done, bf16[4096,256]{1,0:T(8,128)(2,1)S(1)} %copy-done.11), kind=kOutput, calls=%fused_computation | convolution fusion | flops 4295491584 | bytes 19922944 | tf_op jit(solution)/shard_map/dot_general | solution.py:529
  334.6 28.5 %all_to_all.19 = bf16[16,128,256]{2,1,0:T(8,128)(2,1)S(1)} all-to-all(bf16[16,128,256]{2,1,0:T(8,128)(2,1)S(1)} %bitcast.40), channel_id=1, replica_groups=mesh['ctx'=16,'grp'=2] {'ctx'}, dimensions={0} | all-to-all | bytes 2097152 | tf_op jit(solution)/shard_map/all_to_all | solution.py:533
  367.2 10.6 %fusion.5 = f32[4096,256]{1,0:T(8,128)} fusion(bf16[2048,4096]{1,0:T(8,128)(2,1)} %all-gather.2.cloned.1.call-done, bf16[2048,256]{1,0:T(8,128)(2,1)S(1)} %bitcast.39), kind=kOutput, calls=%fused_computation.14 | convolution fusion | flops 4294967296 | bytes 22020096 | tf_op jit(solution)/shard_map/dot_general | solution.py:530
  377.8 7.2 %reduce-scatter.2.cloned.1.call-done = bf16[128,2048]{1,0:T(8,128)(2,1)} async-done(((bf16[128,4096]{1,0:T(8,128)(2,1)}), bf16[128,2048]{1,0:T(8,128)(2,1)}) %reduce-scatter.2.cloned.1.call-update) | async-done | bytes 524304 | tf_op jit(solution)/shard_map/reduce_scatter | solution.py:534
  (78 shorter events, 17.0 us)
Async XLA Ops:
  7.2 5.4 %copy-start.20 = (bf16[256,128]{1,0:T(8,128)(2,1)S(1)}, bf16[256,128]{1,0:T(8,128)(2,1)}, u32[]{:S(2)}) copy-start(bf16[256,128]{1,0:T(8,128)(2,1)} %param.14) | copy-start | bytes 196612
  7.2 5.8 %copy-start.10 = (bf16[4096,256]{1,0:T(8,128)(2,1)S(1)}, bf16[4096,256]{1,0:T(8,128)(2,1)}, u32[]{:S(2)}) copy-start(bf16[4096,256]{1,0:T(8,128)(2,1)} %refs_1_.3) | copy-start | bytes 6291460
  7.2 319.1 %all-gather.2.cloned.1.call-start = ((), (), s32[]{:S(2)}) async-start(), calls=%async_computation.2 | async-start | bytes 17825792 | tf_op jit(solution)/shard_map/all_gather | solution.py:493
  10.2 153.2 %collective-permute-start.2 = (bf16[128,4096]{1,0:T(8,128)(2,1)}, bf16[128,4096]{1,0:T(8,128)(2,1)S(1)}, u32[]{:S(2)}, u32[]{:S(2)}) collective-permute-start(bf16[128,4096]{1,0:T(8,128)(2,1)} %fusion.1), channel_id=1, source_target_pairs={{0,2},{2,4},{4,6},{6,8},{8,10},{10,12},{12,14},{14,16},{16,18},{18... | collective-permute-start | bytes 3145736 | tf_op jit(solution)/shard_map/ppermute | solution.py:478
  14.0 150.3 %copy-start.1 = (bf16[3,128,4096]{2,1,0:T(8,128)(2,1)S(1)}, bf16[3,128,4096]{2,1,0:T(8,128)(2,1)}, u32[]{:S(2)}) copy-start(bf16[3,128,4096]{2,1,0:T(8,128)(2,1)} %inputs_ref.3) | copy-start | bytes 9437188
  14.0 150.3 %copy-start.16 = (f32[4096]{0:T(1024)S(1)}, f32[4096]{0:T(1024)}, u32[]{:S(2)}) copy-start(f32[4096]{0:T(1024)} %param.15) | copy-start | bytes 49156
  163.3 11.2 %copy-start.4 = (bf16[128,4096]{1,0:T(8,128)(2,1)}, bf16[128,4096]{1,0:T(8,128)(2,1)S(1)}, u32[]{:S(2)}) copy-start(bf16[128,4096]{1,0:T(8,128)(2,1)S(1)} %get-tuple-element.26.upstream_ref) | copy-start | bytes 3145732
  163.3 11.2 %copy-start.6 = (bf16[2,8,128,256]{3,2,1,0:T(8,128)(2,1)}, bf16[2,8,128,256]{3,2,1,0:T(8,128)(2,1)S(1)}, u32[]{:S(2)}) copy-start(bf16[2,8,128,256]{3,2,1,0:T(8,128)(2,1)S(1)} %get-tuple-element.36) | copy-start | bytes 3145732
  164.4 1.2 copy-start.13
  165.6 11.3 %copy-start = (bf16[3,128,4096]{2,1,0:T(8,128)(2,1)S(1)}, bf16[3,128,4096]{2,1,0:T(8,128)(2,1)}, u32[]{:S(2)}) copy-start(bf16[3,128,4096]{2,1,0:T(8,128)(2,1)} %refs_0_.2) | copy-start | bytes 9437188
  175.5 1.3 copy-start.18
  176.8 9.8 %copy-start.21 = (bf16[256,7]{0,1:T(8,128)(2,1)S(1)}, bf16[256,7]{0,1:T(8,128)(2,1)}, u32[]{:S(2)}) copy-start(bf16[256,7]{0,1:T(8,128)(2,1)} %param.11) | copy-start | bytes 10756
  176.8 208.1 %reduce-scatter.2.cloned.1.call-start = ((), (), s32[]{:S(2)}) async-start(), calls=%async_computation.3 | async-start | bytes 1572864 | tf_op jit(solution)/shard_map/reduce_scatter | solution.py:534
  177.5 13.8 %copy-start.9 = (f32[4096]{0:T(1024)S(1)}, f32[4096]{0:T(1024)}, u32[]{:S(2)}) copy-start(f32[4096]{0:T(1024)} %param.12) | copy-start | bytes 49156
  177.5 12.1 %collective-permute-start = (bf16[8,4096]{1,0:T(8,128)(2,1)}, bf16[8,4096]{1,0:T(8,128)(2,1)}, u32[]{:S(2)}, u32[]{:S(2)}) collective-permute-start(bf16[8,4096]{1,0:T(8,128)(2,1)} %fusion.3), channel_id=1, source_target_pairs={{0,2},{2,4},{4,6},{6,8},{8,10},{10,12},{12,14},{14,16},{16,18},{18... | collective-permute-start | bytes 196616 | tf_op jit(solution)/shard_map/ppermute | solution.py:479
  182.4 21.1 %collective-permute-start.3 = (bf16[128,4096]{1,0:T(8,128)(2,1)}, bf16[128,4096]{1,0:T(8,128)(2,1)}, u32[]{:S(2)}, u32[]{:S(2)}) collective-permute-start(bf16[128,4096]{1,0:T(8,128)(2,1)} %fusion), channel_id=1, source_target_pairs={{2,0},{4,2},{6,4},{8,6},{10,8},{12,10},{14,12},{16,14},{18,16},{20... | collective-permute-start | bytes 3145736 | tf_op jit(solution)/shard_map/ppermute | solution.py:502
  185.1 5.4 %collective-permute-start.1 = (bf16[8,4096]{1,0:T(8,128)(2,1)}, bf16[8,4096]{1,0:T(8,128)(2,1)}, u32[]{:S(2)}, u32[]{:S(2)}) collective-permute-start(bf16[8,4096]{1,0:T(8,128)(2,1)} %fusion.2), channel_id=1, source_target_pairs={{2,0},{4,2},{6,4},{8,6},{10,8},{12,10},{14,12},{16,14},{18,16},{20... | collective-permute-start | bytes 196616 | tf_op jit(solution)/shard_map/ppermute | solution.py:482
  191.4 1.2 copy-start.3
  203.4 1.9 copy-start.2
  205.4 1.2 copy-start.5
  206.6 1.2 copy-start.14
  208.5 1.6 copy-start.19
  232.1 94.2 %copy-start.11 = (bf16[4096,256]{1,0:T(8,128)(2,1)S(1)}, bf16[4096,256]{1,0:T(8,128)(2,1)}, u32[]{:S(2)}) copy-start(bf16[4096,256]{1,0:T(8,128)(2,1)} %refs_1_.3) | copy-start | bytes 6291460
  334.6 29.6 %copy-start.7 = (bf16[2,8,128,256]{3,2,1,0:T(8,128)(2,1)S(1)}, bf16[2,8,128,256]{3,2,1,0:T(8,128)(2,1)}, u32[]{:S(2)}) copy-start(bf16[2,8,128,256]{3,2,1,0:T(8,128)(2,1)} %copy-done.6) | copy-start | bytes 3145732
  (4 other events, 3.7 us)
Sparse Core Ops, SparseCore 0:
  177.0 149.3 all-gather.1
  364.3 20.5 reduce-scatter.1

commit v3 on v2

--- a/solution.py
+++ b/solution.py
@@ -347,7 +347,7 @@
     rows = cotangent.shape[0]
     channels, width = weight.shape
     hops, half = n // 2, rows // 2
-    tile = min(512, channels)
+    tile = min(1024, channels)
     dma = pltpu.SemaphoreType.DMA
 
     def kernel(*refs):

time: 393 us -> 393 us (level)
  transfers between devices with their start and end apart: 6 -> 6, of which waited for: 2 -> 3; matrix products, arithmetic and copies ran while one was open for 7% -> 7% of each run, Pallas kernels for 64% -> 64%
where the time goes in v3:
time: 393 us; the launch traced here: 392 us
  Pallas kernels  259 us (66%)
  waiting for transfers between devices  28.7 us (7%)
  blocking collectives  28.5 us (7%)
  local copies, waits for them, and re-layouts  22.5 us (6%)
  matrix products  18.8 us (5%)
  between operations  14.4 us (4%)
  other arithmetic  13 us (3%)
  starting transfers between devices  7.26 us (2%)
    pallas_call x1, Pallas kernels, ring_upstream(): pl.pallas_call(kernel, in_specs=[vmem, vmem], out_specs=[vmem, vmem], out...  149 us
    pallas_call x1, Pallas kernels, sum_over_ctx(): pl.pallas_call(kernel, in_specs=[vmem], out_specs=vmem, out_shape=jax.Sha...  69.2 us
    all_to_all x1, blocking collectives, on_device(): lax.all_to_all(partial_value, 'ctx', split_axis=0, concat_axis=1, tiled=T...  28.5 us
    pallas_call x1, Pallas kernels, mr_backward(): pl.pallas_call(mr_backward_kernel, grid=(channels // LANES,), in_specs=[c...  21.9 us
    all_gather x1, waiting for transfers between devices, on_device(): gathered = lax.all_gather(mixed_mr, 'ctx', axis=0, tiled=True)  21.3 us
    unnamed x45, local copies, waits for them, and re-layouts  14.2 us
    dot_general x1, matrix products, on_device(): lax.dot_general(gathered, columns, (((0,), (0,)), ((), ())), preferred_el...  10.6 us
    pallas_call x1, Pallas kernels, se_operator(): pl.pallas_call(kernel, grid=(channels // LANES,), in_specs=[cube, flat, e...  9.82 us
  transfers between devices with their start and end apart: 6, of which 3 were waited for; matrix products, arithmetic and copies ran while one was open for 7% of the time, Pallas kernels for 64%

profile of v3, /device:TPU:0, one launch (start us, length us, event | category | flops | bytes accessed | tf_op | source)
XLA Modules:
  0.0 391.8 jit_solution(8244316600098002988)
XLA Ops:
  7.2 2.9 fusion.1
  10.2 2.4 collective-permute-start.2
  14.0 148.7 %ring_upstream.1 = (bf16[128,4096]{1,0:T(8,128)(2,1)S(1)}, bf16[2,8,128,256]{3,2,1,0:T(8,128)(2,1)S(1)}) custom-call(bf16[128,2048]{1,0:T(8,128)(2,1)S(1)} %copy-done.15, bf16[4096,256]{1,0:T(8,128)(2,1)S(1)} %copy-done.10), custom_call_target="tpu_custom_call" | custom-call | flops 4294967296 | bytes 314572800 | tf_op jit(solution)/shard_map/ring_upstream/pallas_call | solution.py:357
  163.8 1.2 copy-done.13
  165.1 8.9 %mr_forward.1 = (f32[128,4096]{1,0:T(8,128)S(1)}, bf16[128,4096]{1,0:T(8,128)(2,1)S(1)}) custom-call(bf16[3,128,4096]{2,1,0:T(8,128)(2,1)S(1)} %copy-done.1, bf16[128,4096]{1,0:T(8,128)(2,1)S(1)} %copy-done.13, f32[256,256]{1,0:T(8,128)S(1)} %maximum_maximum_fusion.base_ref, f32[1,4096]{1,0:T(1,128)S(1)} %bitcast.35), custom_call_target="tpu_custom_call" | custom-call | flops 4294967296 | bytes 5767168 | tf_op jit(solution)/shard_map/mr_forward/pallas_call | solution.py:40
  175.0 1.3 copy-done.18
  177.0 2.0 collective-permute-start
  179.0 2.8 fusion
  181.8 1.3 collective-permute-start.3
  183.1 1.5 fusion.2
  184.6 1.5 collective-permute-start.1
  186.1 1.2 broadcast_in_dim.21
  187.3 1.8 reshape.64
  192.4 9.8 %se_operator.1 = (bf16[128,4096]{1,0:T(8,128)(2,1)}, bf16[3,128,4096]{2,1,0:T(8,128)(2,1)}, f32[8,4096]{1,0:T(8,128)S(1)}) custom-call(bf16[3,128,4096]{2,1,0:T(8,128)(2,1)S(1)} %copy-done, bf16[128,4096]{1,0:T(8,128)(2,1)S(1)} %copy-done.3, f32[8,4096]{1,0:T(8,128)S(1)} %convert_element_type.69.refs_2_, f32[8,4096]{1,0:T(8,128)S(1)} %convert_element_type.74.refs_3_, ...), custom_call_target="tpu_custom_call" | custom-call | flops 26214400 | bytes 8388608 | tf_op jit(solution)/shard_map/se_operator/pallas_call | solution.py:168
  203.3 1.9 copy-done.2
  208.3 1.6 copy-done.19
  210.0 21.9 %mr_backward.1 = (bf16[3,128,4096]{2,1,0:T(8,128)(2,1)}, f32[256,8,256]{2,1,0:T(8,128)S(1)}, f32[1,4096]{1,0:T(1,128)S(1)}) custom-call(bf16[3,128,4096]{2,1,0:T(8,128)(2,1)S(1)} %copy-done.2, bf16[128,4096]{1,0:T(8,128)(2,1)S(1)} %copy-done.14, bf16[128,4096]{1,0:T(8,128)(2,1)S(1)} %copy-done.5, bf16[128,4096]{1,0:T(8,128)(2,1)} %collective-permute-done.3.after_ref, ...), custom_call_target="tpu_custom_call" | custom-call | flops 8589934592 | bytes 12582912 | tf_op jit(solution)/shard_map/mr_backward/pallas_call | solution.py:99
  231.9 2.2 add_add_fusion
  235.8 69.2 %sum_over_ctx.1 = f32[16,16,256]{2,1,0:T(8,128)S(1)} custom-call(f32[16,16,256]{2,1,0:T(8,128)S(1)} %concatenate.28.refs_0_), custom_call_target="tpu_custom_call" | custom-call | flops 65536 | bytes 41943040 | tf_op jit(solution)/shard_map/sum_over_ctx/pallas_call | solution.py:444
  305.1 21.3 %all-gather.2.cloned.1.call-done = bf16[2048,4096]{1,0:T(8,128)(2,1)} async-done(((bf16[128,4096]{1,0:T(8,128)(2,1)}), bf16[2048,4096]{1,0:T(8,128)(2,1)}) %all-gather.2.cloned.1.call-update) | async-done | bytes 16777232 | tf_op jit(solution)/shard_map/all_gather | solution.py:493
  326.3 8.2 %convolution_convert_fusion = bf16[2048,256]{1,0:T(8,128)(2,1)S(1)} fusion(bf16[2048,4096]{1,0:T(8,128)(2,1)} %all-gather.2.cloned.1.call-done, bf16[4096,256]{1,0:T(8,128)(2,1)S(1)} %copy-done.11), kind=kOutput, calls=%fused_computation | convolution fusion | flops 4295491584 | bytes 19922944 | tf_op jit(solution)/shard_map/dot_general | solution.py:529
  334.6 28.5 %all_to_all.19 = bf16[16,128,256]{2,1,0:T(8,128)(2,1)S(1)} all-to-all(bf16[16,128,256]{2,1,0:T(8,128)(2,1)S(1)} %bitcast.40), channel_id=1, replica_groups=mesh['ctx'=16,'grp'=2] {'ctx'}, dimensions={0} | all-to-all | bytes 2097152 | tf_op jit(solution)/shard_map/all_to_all | solution.py:533
  367.2 10.6 %fusion.5 = f32[4096,256]{1,0:T(8,128)} fusion(bf16[2048,4096]{1,0:T(8,128)(2,1)} %all-gather.2.cloned.1.call-done, bf16[2048,256]{1,0:T(8,128)(2,1)S(1)} %bitcast.39), kind=kOutput, calls=%fused_computation.14 | convolution fusion | flops 4294967296 | bytes 22020096 | tf_op jit(solution)/shard_map/dot_general | solution.py:530
  377.8 7.2 %reduce-scatter.2.cloned.1.call-done = bf16[128,2048]{1,0:T(8,128)(2,1)} async-done(((bf16[128,4096]{1,0:T(8,128)(2,1)}), bf16[128,2048]{1,0:T(8,128)(2,1)}) %reduce-scatter.2.cloned.1.call-update) | async-done | bytes 524304 | tf_op jit(solution)/shard_map/reduce_scatter | solution.py:534
  (78 shorter events, 17.4 us)
Async XLA Ops:
  7.2 5.4 %copy-start.20 = (bf16[256,128]{1,0:T(8,128)(2,1)S(1)}, bf16[256,128]{1,0:T(8,128)(2,1)}, u32[]{:S(2)}) copy-start(bf16[256,128]{1,0:T(8,128)(2,1)} %param.14) | copy-start | bytes 196612
  7.2 5.8 %copy-start.10 = (bf16[4096,256]{1,0:T(8,128)(2,1)S(1)}, bf16[4096,256]{1,0:T(8,128)(2,1)}, u32[]{:S(2)}) copy-start(bf16[4096,256]{1,0:T(8,128)(2,1)} %refs_1_.3) | copy-start | bytes 6291460
  7.2 319.1 %all-gather.2.cloned.1.call-start = ((), (), s32[]{:S(2)}) async-start(), calls=%async_computation.2 | async-start | bytes 17825792 | tf_op jit(solution)/shard_map/all_gather | solution.py:493
  10.2 152.7 %collective-permute-start.2 = (bf16[128,4096]{1,0:T(8,128)(2,1)}, bf16[128,4096]{1,0:T(8,128)(2,1)S(1)}, u32[]{:S(2)}, u32[]{:S(2)}) collective-permute-start(bf16[128,4096]{1,0:T(8,128)(2,1)} %fusion.1), channel_id=1, source_target_pairs={{0,2},{2,4},{4,6},{6,8},{8,10},{10,12},{12,14},{14,16},{16,18},{18... | collective-permute-start | bytes 3145736 | tf_op jit(solution)/shard_map/ppermute | solution.py:478
  14.0 149.8 %copy-start.1 = (bf16[3,128,4096]{2,1,0:T(8,128)(2,1)S(1)}, bf16[3,128,4096]{2,1,0:T(8,128)(2,1)}, u32[]{:S(2)}) copy-start(bf16[3,128,4096]{2,1,0:T(8,128)(2,1)} %inputs_ref.3) | copy-start | bytes 9437188
  14.0 149.8 %copy-start.16 = (f32[4096]{0:T(1024)S(1)}, f32[4096]{0:T(1024)}, u32[]{:S(2)}) copy-start(f32[4096]{0:T(1024)} %param.15) | copy-start | bytes 49156
  162.8 11.2 %copy-start.4 = (bf16[128,4096]{1,0:T(8,128)(2,1)}, bf16[128,4096]{1,0:T(8,128)(2,1)S(1)}, u32[]{:S(2)}) copy-start(bf16[128,4096]{1,0:T(8,128)(2,1)S(1)} %get-tuple-element.26.upstream_ref) | copy-start | bytes 3145732
  162.8 11.2 %copy-start.6 = (bf16[2,8,128,256]{3,2,1,0:T(8,128)(2,1)}, bf16[2,8,128,256]{3,2,1,0:T(8,128)(2,1)S(1)}, u32[]{:S(2)}) copy-start(bf16[2,8,128,256]{3,2,1,0:T(8,128)(2,1)S(1)} %get-tuple-element.36) | copy-start | bytes 3145732
  163.8 1.2 copy-start.13
  165.1 11.3 %copy-start = (bf16[3,128,4096]{2,1,0:T(8,128)(2,1)S(1)}, bf16[3,128,4096]{2,1,0:T(8,128)(2,1)}, u32[]{:S(2)}) copy-start(bf16[3,128,4096]{2,1,0:T(8,128)(2,1)} %refs_0_.2) | copy-start | bytes 9437188
  175.0 1.3 copy-start.18
  176.3 9.8 %copy-start.21 = (bf16[256,7]{0,1:T(8,128)(2,1)S(1)}, bf16[256,7]{0,1:T(8,128)(2,1)}, u32[]{:S(2)}) copy-start(bf16[256,7]{0,1:T(8,128)(2,1)} %param.11) | copy-start | bytes 10756
  176.3 208.7 %reduce-scatter.2.cloned.1.call-start = ((), (), s32[]{:S(2)}) async-start(), calls=%async_computation.3 | async-start | bytes 1572864 | tf_op jit(solution)/shard_map/reduce_scatter | solution.py:534
  177.0 14.2 %copy-start.9 = (f32[4096]{0:T(1024)S(1)}, f32[4096]{0:T(1024)}, u32[]{:S(2)}) copy-start(f32[4096]{0:T(1024)} %param.12) | copy-start | bytes 49156
  177.0 12.2 %collective-permute-start = (bf16[8,4096]{1,0:T(8,128)(2,1)}, bf16[8,4096]{1,0:T(8,128)(2,1)}, u32[]{:S(2)}, u32[]{:S(2)}) collective-permute-start(bf16[8,4096]{1,0:T(8,128)(2,1)} %fusion.3), channel_id=1, source_target_pairs={{0,2},{2,4},{4,6},{6,8},{8,10},{10,12},{12,14},{14,16},{16,18},{18... | collective-permute-start | bytes 196616 | tf_op jit(solution)/shard_map/ppermute | solution.py:479
  181.8 21.4 %collective-permute-start.3 = (bf16[128,4096]{1,0:T(8,128)(2,1)}, bf16[128,4096]{1,0:T(8,128)(2,1)}, u32[]{:S(2)}, u32[]{:S(2)}) collective-permute-start(bf16[128,4096]{1,0:T(8,128)(2,1)} %fusion), channel_id=1, source_target_pairs={{2,0},{4,2},{6,4},{8,6},{10,8},{12,10},{14,12},{16,14},{18,16},{20... | collective-permute-start | bytes 3145736 | tf_op jit(solution)/shard_map/ppermute | solution.py:502
  184.6 5.7 %collective-permute-start.1 = (bf16[8,4096]{1,0:T(8,128)(2,1)}, bf16[8,4096]{1,0:T(8,128)(2,1)}, u32[]{:S(2)}, u32[]{:S(2)}) collective-permute-start(bf16[8,4096]{1,0:T(8,128)(2,1)} %fusion.2), channel_id=1, source_target_pairs={{2,0},{4,2},{6,4},{8,6},{10,8},{12,10},{14,12},{16,14},{18,16},{20... | collective-permute-start | bytes 196616 | tf_op jit(solution)/shard_map/ppermute | solution.py:482
  191.2 1.2 copy-start.3
  203.2 1.9 copy-start.2
  205.2 1.2 copy-start.5
  206.4 1.2 copy-start.14
  208.3 1.6 copy-start.19
  231.9 94.4 %copy-start.11 = (bf16[4096,256]{1,0:T(8,128)(2,1)S(1)}, bf16[4096,256]{1,0:T(8,128)(2,1)}, u32[]{:S(2)}) copy-start(bf16[4096,256]{1,0:T(8,128)(2,1)} %refs_1_.3) | copy-start | bytes 6291460
  334.6 29.6 %copy-start.7 = (bf16[2,8,128,256]{3,2,1,0:T(8,128)(2,1)S(1)}, bf16[2,8,128,256]{3,2,1,0:T(8,128)(2,1)}, u32[]{:S(2)}) copy-start(bf16[2,8,128,256]{3,2,1,0:T(8,128)(2,1)} %copy-done.6) | copy-start | bytes 3145732
  (4 other events, 3.7 us)
Sparse Core Ops, SparseCore 0:
  176.4 149.8 all-gather.1
  364.3 20.5 reduce-scatter.1
